TPU v7x, 128 devices: a whole 4x4x4 slice. The times are simulated.
128 devices in a mesh: user: 16 (over z, x), item: 8 (over y, core).
Axes of the slice: x: 4, y: 4, z: 4, core: 2. Of those that a mesh axis runs over, the one named last changes fastest.
Arguments:
- cand_ids: int32 [128, 1024], P(('user', 'item')), may hold values from 0 to 524287, as said below
- hist_ids: int32 [128, 1024], P(('user', 'item')), may hold values from 0 to 524287, as said below
- hist_len: int32 [128], P(('user', 'item')), may hold values from 1 to 1024, as said below
- teacher: float32 [128, 1024], P(('user', 'item')), may hold values from -16 to 16
- table: bfloat16 [524288, 256], P(('user', 'item')), may hold values from -6 to 6
- w_query: bfloat16 [256, 256], replicated, may hold values from -0.375 to 0.375
- w_key: bfloat16 [256, 256], replicated, may hold values from -0.375 to 0.375
- w_value: bfloat16 [256, 256], replicated, may hold values from -0.375 to 0.375
Outputs:
- grad_table: float32 [524288, 256], P(('user', 'item'))
Inputs may be any that keep to these rules, and one draw needn't show every extreme that they name: `hist_ids`: ids are owned in blocks of 4096: id // 4096 is the owning device in the order of user+item. Of the 2048 candidate and history ids of one device's users together, at most 40 fall in one owner's block; in every draw some owner receives exactly 40 from every device. `cand_ids`: the same bound as for hist_ids holds for candidate and history ids together. `hist_len`: some user's history has exactly 1024 behaviours; history slots at or beyond a user's length are ignored.
All inputs are finite; a program needn't handle non-finite values.
Results may differ from a plain program's by a relative error of at most 0.022.
Values may be sent and summed in bfloat16 or wider, within the bound.
A program may use at most 64 MiB of HBM per device.

v0:
```python
import math

import jax
import jax.numpy as jnp
from jax import lax
from jax.sharding import PartitionSpec as P

HEADS = 4
GRAD_SCALE = 1024


def project(hist_full, w_key, w_value):
    hist_half = hist_full.astype(jnp.bfloat16)
    keys = jnp.dot(hist_half, w_key, preferred_element_type=jnp.float32).astype(jnp.bfloat16)
    values = jnp.dot(hist_half, w_value, preferred_element_type=jnp.float32).astype(jnp.bfloat16)
    return (keys, values)


def block_loss(cand_rows, keys, values, length, target, w_query):
    cand_half = cand_rows.astype(jnp.bfloat16)
    query = jnp.dot(cand_half, w_query, preferred_element_type=jnp.float32).astype(jnp.bfloat16)
    q_heads = query.reshape(query.shape[0], HEADS, -1)
    k_heads = keys.reshape(keys.shape[0], HEADS, -1)
    v_heads = values.reshape(values.shape[0], HEADS, -1)
    score = jnp.einsum("jhd,thd->hjt", q_heads, k_heads, preferred_element_type=jnp.float32)
    score = score / math.sqrt(q_heads.shape[2])
    live = jnp.arange(k_heads.shape[0], dtype=jnp.int32) < length
    raised = jnp.where(live[None, None, :], jnp.exp(score), 0.0)
    attn = (raised / jnp.sum(raised, axis=2, keepdims=True)).astype(jnp.bfloat16)
    attended = jnp.einsum("hjt,thd->jhd", attn, v_heads, preferred_element_type=jnp.float32)
    attended = attended.reshape(attended.shape[0], -1)
    logit = jnp.sum(attended * cand_rows, axis=1) / math.sqrt(attended.shape[1])
    soft_target = jax.nn.sigmoid(target)
    return GRAD_SCALE * jnp.sum(jax.nn.softplus(logit) - soft_target * logit)


def user_grads(cand_rows, hist_rows, length, target, w_query, w_key, w_value):

    def projected(hist_full):
        return project(hist_full, w_key, w_value)

    (keys, values), proj_back = jax.vjp(projected, hist_rows.astype(jnp.float32))
    cand_count, width = cand_rows.shape
    block = min(512, cand_count)
    cand_blocks = cand_rows.astype(jnp.float32).reshape(cand_count // block, block, width)
    target_blocks = target.reshape(cand_count // block, block)

    def advance(carry, item):
        cand_part, target_part = item

        def scaled(cand_full, key_part, value_part):
            return block_loss(cand_full, key_part, value_part, length, target_part, w_query)

        loss_value, pullback = jax.vjp(scaled, cand_part, keys, values)
        grad_cand, grad_keys, grad_values = pullback(jnp.ones_like(loss_value))
        summed = (
            carry[0] + grad_keys.astype(jnp.float32),
            carry[1] + grad_values.astype(jnp.float32),
        )
        return (summed, grad_cand)

    start = (jnp.zeros(keys.shape, jnp.float32), jnp.zeros(values.shape, jnp.float32))
    (key_total, value_total), grad_cand = lax.scan(advance, start, (cand_blocks, target_blocks))
    (grad_hist,) = proj_back((key_total.astype(jnp.bfloat16), value_total.astype(jnp.bfloat16)))
    return (grad_cand.reshape(cand_count, width), grad_hist)


def body(cand_ids, hist_ids, hist_len, teacher, table, w_query, w_key, w_value):
    rows_dev, width = table.shape
    users_here, cand = cand_ids.shape
    user_count = lax.axis_size("user")
    item_count = lax.axis_size("item")
    devices = user_count * item_count
    wanted = jnp.concatenate([cand_ids, hist_ids], axis=1).reshape(-1)
    slots = wanted.shape[0]
    capacity = 5 * (slots // devices) // 2
    owner = wanted // rows_dev
    local = wanted % rows_dev
    onehot = (owner[:, None] == jnp.arange(devices, dtype=jnp.int32)[None, :]).astype(jnp.int32)
    rank = jnp.sum(jnp.cumsum(onehot, axis=0) * onehot, axis=1) - 1
    place = owner * capacity + rank
    request = jnp.zeros((devices * capacity,), jnp.int32).at[place].set(local)
    asked = lax.all_to_all(
        request.reshape(devices, capacity),
        ("user", "item"),
        split_axis=0,
        concat_axis=0,
        tiled=True,
    )
    found = table[asked]
    asked, fetched = (
        asked,
        lax.all_to_all(found, ("user", "item"), split_axis=0, concat_axis=0, tiled=True),
    )
    rows = fetched.reshape(devices * capacity, width)[place].reshape(users_here, -1, width)
    cand_rows = rows[:, :cand]
    hist_rows = rows[:, cand:]

    def one_user(item):
        cand_part, hist_part, length, target = item
        return user_grads(cand_part, hist_part, length, target, w_query, w_key, w_value)

    grad_cand, grad_hist = lax.map(one_user, (cand_rows, hist_rows, hist_len, teacher))
    grad_flat = jnp.concatenate([grad_cand, grad_hist], axis=1).reshape(-1, width)
    outgoing = jnp.zeros((devices * capacity, width), jnp.float32).at[place].set(grad_flat)
    arrived = lax.all_to_all(
        outgoing.reshape(devices, capacity, width),
        ("user", "item"),
        split_axis=0,
        concat_axis=0,
        tiled=True,
    )
    grad_table = jnp.zeros((rows_dev, width), jnp.float32)
    return grad_table.at[asked.reshape(-1)].add(arrived.reshape(-1, width))


def solution(mesh):
    placed = (
        P(("user", "item"), None),
        P(("user", "item"), None),
        P(("user", "item")),
        P(("user", "item"), None),
        P(("user", "item"), None),
        P(),
        P(),
        P(),
    )
    return jax.shard_map(
        body, mesh=mesh, in_specs=placed, out_specs=P(("user", "item"), None), check_vma=False
    )
```

profile of v0, /device:TPU:1, one launch (start us, length us, event | category | flops | bytes accessed | tf_op | source)
XLA Modules:
  0.0 294.4 jit_solution(2046072194719294523)
XLA Ops:
  0.0 0.8 constant_dynamic-update-slice_fusion.1
  0.8 0.7 constant_dynamic-update-slice_fusion
  1.7 0.3 fusion.38
  2.1 0.3 copy.22
  2.5 0.6 fusion.37
  3.2 8.1 %scatter_custom_fusion = s32[5120]{0:T(1024)S(1)} fusion(s32[2048]{0:T(1024)S(1)} %bitcast.176, s32[2048]{0:T(1024)S(1)} %get-tuple-element.183, s32[]{:T(128)} %constant.91.clone.1), kind=kCustom, calls=%fused_computation.95 | custom fusion | bytes 20484 | tf_op jit(solution)/shard_map/scatter | solution.py:82
  11.4 20.9 %all_to_all.22 = s32[128,1,40]{2,1,0:T(1,128)S(1)} all-to-all(s32[128,1,40]{2,1,0:T(1,128)S(1)} %bitcast.172), channel_id=1, replica_groups=mesh['user'=16,'item'=8] {'user','item'}, dimensions={0} | all-to-all | bytes 40960 | tf_op jit(solution)/shard_map/all_to_all | solution.py:83
  32.3 0.6 copy-done.12
  33.0 21.1 %gather_fusion = bf16[5120,256]{1,0:T(8,128)(2,1)} fusion(bf16[4096,256]{1,0:T(8,128)(2,1)S(1)} %copy-done, s32[5120]{0:T(1024)S(1)} %broadcast_clamp_fusion), kind=kCustom, calls=%fused_computation | custom fusion | bytes 5263360 | tf_op jit(solution)/shard_map/gather | solution.py:90
  54.2 5.4 %all-to-all-start.1 = ((bf16[128,40,256]{2,1,0:T(8,128)(2,1)}), bf16[128,40,256]{2,1,0:T(8,128)(2,1)}, u32[]{:S(2)}, u32[]{:S(2)}) async-start(bf16[128,40,256]{2,1,0:T(8,128)(2,1)} %bitcast.165), calls=%async_computation.1 | async-start | bytes 5242880 | tf_op jit(solution)/shard_map/all_to_all | solution.py:93
  59.6 0.6 broadcast.296
  60.1 0.7 reduce.8
  60.9 34.6 %all-to-all-done.1 = bf16[128,40,256]{2,1,0:T(8,128)(2,1)} async-done(((bf16[128,40,256]{2,1,0:T(8,128)(2,1)}), bf16[128,40,256]{2,1,0:T(8,128)(2,1)}, u32[]{:S(2)}, u32[]{:S(2)}) %all-to-all-start.1) | async-done | bytes 2621472 | tf_op jit(solution)/shard_map/all_to_all | solution.py:93
  95.5 8.8 %gather_fusion.1 = bf16[2048,256]{1,0:T(8,128)(2,1)S(1)} fusion(bf16[5120,256]{1,0:T(8,128)(2,1)} %bitcast.13, s32[2048]{0:T(1024)S(1)} %broadcast_clamp_fusion.1), kind=kCustom, calls=%fused_computation.1 | custom fusion | bytes 2105344 | tf_op jit(solution)/shard_map/gather | solution.py:95
  104.3 0.8 slice.22
  105.1 1.1 convolution_convert_fusion.8
  106.2 2.1 copy.26
  108.2 1.1 convolution_convert_fusion.9
  109.3 1.2 copy.25
  110.6 2.1 convert.6
  112.7 63.1 %while.25 = (s32[]{:T(128)}, f32[1024,256]{0,1:T(8,128)}, f32[1024,256]{0,1:T(8,128)}, f32[2,512,256]{2,1,0:T(8,128)}, s32[]{:T(128)}, /*index=5*/f32[2,512]{1,0...) while((s32[]{:T(128)}, f32[1024,256]{0,1:T(8,128)}, ...), condition=%wide.region_8.9_spmd.clone, body=%wide.region_4.8_spmd.clone.sunk | while | flops 1794125824 | bytes 153239120 | solution.py:63
  112.7 0.6 iota_compare_fusion.5
  113.5 1.1 constant_dynamic-slice_fusion.2
  115.1 3.0 %fusion.106 = (f32[4,512]{1,0:T(4,128)S(1)}, f32[4,512,1024]{2,1,0:T(8,128)S(1)}) fusion(pred[1024]{0:T(1024)(128)(4,1)S(1)} %iota_compare_fusion.5, bf16[512,4,64]{0,2,1:T(8,128)(2,1)S(1)} %bitcast.160, bf16[1024,4,64]{0,2,1:T(8,128)(2,1)} %bitcast.163), kind=kOutput, calls=%fused_computation.16.clone.1 | convolution fusion | flops 274724864 | bytes 9184256 | tf_op jit(solution)/shard_map/while/body/eval_jaxpr/while/body/eval_jaxpr/jvp(jhd,thd->hjt)/dot_general | solution.py:25
  118.1 0.6 multiply_divide_fusion.2
  118.7 1.8 divide_convert_fusion.2
  120.6 0.7 copy-done.1
  121.3 3.2 %fusion.107 = (f32[512]{0:T(512)S(1)}, f32[4,512,64]{1,2,0:T(8,128)}) fusion(f32[512,4,64]{0,2,1:T(8,128)S(1)} %bitcast.155, bf16[4,512,1024]{2,1,0:T(8,128)(2,1)S(1)} %divide_convert_fusion.2, bf16[1024,4,64]{0,2,1:T(8,128)(2,1)} %bitcast.150), kind=kOutput, calls=%fused_computation.34.clone.1 | convolution fusion | flops 268697088 | bytes 5769216 | tf_op jit(solution)/shard_map/while/body/eval_jaxpr/while/body/eval_jaxpr/jvp(hjt,thd->jhd)/dot_general | solution.py:30
  124.5 1.8 fusion.109
  126.4 1.2 copy.31
  127.6 6.1 %fusion.110 = (f32[4,512]{1,0:T(4,128)S(1)}, bf16[4,512,1024]{2,1,0:T(8,128)(2,1)S(1)}) fusion(f32[4,512,1024]{2,1,0:T(8,128)} %copy-done.1, f32[4,512]{1,0:T(4,128)} %multiply_divide_fusion.2, pred[1024]{0:T(1024)(128)(4,1)} %copy-done.16, bf16[1024,4,64]{0,2,1:T(8,128)(2,1)} %bitcast.150, f32[512,4,64]{0,2,1:T(8,128)S(1)} %bitcast.157, ...), kind=kOutput, calls=%fused_computation.12.clone.1 | convolution fusion | flops 283244544 | bytes 13650944 | tf_op jit(solution)/shard_map/while/body/eval_jaxpr/while/body/eval_jaxpr/transpose(jvp(hjt,thd->jhd))/dot_general | solution.py:30
  133.7 5.1 %fusion.111 = bf16[4,512,1024]{2,1,0:T(8,128)(2,1)S(1)} fusion(bf16[4,512,1024]{2,1,0:T(8,128)(2,1)S(1)} %get-tuple-element.257, f32[4,512,1024]{2,1,0:T(8,128)} %copy-done.1, f32[4,512]{1,0:T(4,128)S(1)} %neg.24, f32[4,512]{1,0:T(4,128)S(1)} %get-tuple-element.255, pred[1024]{0:T(1024)(128)(4,1)S(1)} %copy-done.17), kind=kLoop, calls=%fused_computation.10.clone.1 | loop fusion | flops 16777216 | bytes 16794624 | tf_op jit(solution)/shard_map/while/body/eval_jaxpr/while/body/eval_jaxpr/transpose(jvp())/div | solution.py:26
  138.9 1.4 fusion.113
  140.3 0.9 fusion.112
  141.2 0.7 bitcast_add_fusion.3
  142.2 0.7 copy-done.4
  142.8 0.4 copy-done.6
  143.3 1.0 copy-done.11
  144.2 0.6 iota_compare_fusion.5
  145.1 1.1 constant_dynamic-slice_fusion.2
  146.6 3.0 %fusion.106 = (f32[4,512]{1,0:T(4,128)S(1)}, f32[4,512,1024]{2,1,0:T(8,128)S(1)}) fusion(pred[1024]{0:T(1024)(128)(4,1)S(1)} %iota_compare_fusion.5, bf16[512,4,64]{0,2,1:T(8,128)(2,1)S(1)} %bitcast.160, bf16[1024,4,64]{0,2,1:T(8,128)(2,1)} %bitcast.163), kind=kOutput, calls=%fused_computation.16.clone.1 | convolution fusion | flops 274724864 | bytes 9184256 | tf_op jit(solution)/shard_map/while/body/eval_jaxpr/while/body/eval_jaxpr/jvp(jhd,thd->hjt)/dot_general | solution.py:25
  149.6 0.6 multiply_divide_fusion.2
  150.3 1.8 divide_convert_fusion.2
  152.1 0.7 copy-done.1
  152.8 3.2 %fusion.107 = (f32[512]{0:T(512)S(1)}, f32[4,512,64]{1,2,0:T(8,128)}) fusion(f32[512,4,64]{0,2,1:T(8,128)S(1)} %bitcast.155, bf16[4,512,1024]{2,1,0:T(8,128)(2,1)S(1)} %divide_convert_fusion.2, bf16[1024,4,64]{0,2,1:T(8,128)(2,1)} %bitcast.150), kind=kOutput, calls=%fused_computation.34.clone.1 | convolution fusion | flops 268697088 | bytes 5769216 | tf_op jit(solution)/shard_map/while/body/eval_jaxpr/while/body/eval_jaxpr/jvp(hjt,thd->jhd)/dot_general | solution.py:30
  156.1 1.8 fusion.109
  157.9 1.2 copy.31
  159.2 6.1 %fusion.110 = (f32[4,512]{1,0:T(4,128)S(1)}, bf16[4,512,1024]{2,1,0:T(8,128)(2,1)S(1)}) fusion(f32[4,512,1024]{2,1,0:T(8,128)} %copy-done.1, f32[4,512]{1,0:T(4,128)} %multiply_divide_fusion.2, pred[1024]{0:T(1024)(128)(4,1)} %copy-done.16, bf16[1024,4,64]{0,2,1:T(8,128)(2,1)} %bitcast.150, f32[512,4,64]{0,2,1:T(8,128)S(1)} %bitcast.157, ...), kind=kOutput, calls=%fused_computation.12.clone.1 | convolution fusion | flops 283244544 | bytes 13650944 | tf_op jit(solution)/shard_map/while/body/eval_jaxpr/while/body/eval_jaxpr/transpose(jvp(hjt,thd->jhd))/dot_general | solution.py:30
  165.3 5.1 %fusion.111 = bf16[4,512,1024]{2,1,0:T(8,128)(2,1)S(1)} fusion(bf16[4,512,1024]{2,1,0:T(8,128)(2,1)S(1)} %get-tuple-element.257, f32[4,512,1024]{2,1,0:T(8,128)} %copy-done.1, f32[4,512]{1,0:T(4,128)S(1)} %neg.24, f32[4,512]{1,0:T(4,128)S(1)} %get-tuple-element.255, pred[1024]{0:T(1024)(128)(4,1)S(1)} %copy-done.17), kind=kLoop, calls=%fused_computation.10.clone.1 | loop fusion | flops 16777216 | bytes 16794624 | tf_op jit(solution)/shard_map/while/body/eval_jaxpr/while/body/eval_jaxpr/transpose(jvp())/div | solution.py:26
  170.5 1.4 fusion.113
  171.9 0.9 fusion.112
  172.8 0.7 bitcast_add_fusion.3
  173.5 0.3 fusion.114
  173.7 0.7 copy-done.4
  174.4 0.4 copy-done.6
  174.8 1.0 copy-done.11
  175.8 1.6 convolution_convert_fusion.6
  177.4 1.6 fusion.36
  178.9 12.5 %scatter_custom_fusion.1 = f32[5120,256]{1,0:T(8,128)} fusion(s32[2048]{0:T(1024)} %bitcast.178, f32[]{:T(128)} %constant.90.clone.1, f32[1,1024,256]{2,1,0:T(8,128)S(1)} %fusion.36, f32[]{:T(128)} %constant.107, f32[1,1024,256]{2,1,0:T(8,128)} %bitcast.170), kind=kCustom, calls=%fused_computation.53 | custom fusion | flops 524288 | bytes 7341056 | tf_op jit(solution)/shard_map/scatter | solution.py:105
  191.4 5.6 %all-to-all-start.2 = ((f32[128,40,256]{2,1,0:T(8,128)}), f32[128,40,256]{2,1,0:T(8,128)}, u32[]{:S(2)}, u32[]{:S(2)}) async-start(f32[128,40,256]{2,1,0:T(8,128)} %bitcast.162), calls=%async_computation.2 | async-start | bytes 10485760 | tf_op jit(solution)/shard_map/all_to_all | solution.py:106
  197.1 0.5 broadcast.295
  197.6 0.8 reduce.7
  198.6 62.8 %all-to-all-done.2 = f32[128,40,256]{2,1,0:T(8,128)} async-done(((f32[128,40,256]{2,1,0:T(8,128)}), f32[128,40,256]{2,1,0:T(8,128)}, u32[]{:S(2)}, u32[]{:S(2)}) %all-to-all-start.2) | async-done | bytes 5242912 | tf_op jit(solution)/shard_map/all_to_all | solution.py:106
  261.3 33.1 %scatter_custom_fusion.2 = f32[4096,256]{1,0:T(8,128)} fusion(s32[5120]{0:T(1024)S(1)} %bitcast.180, f32[5120,256]{1,0:T(8,128)} %bitcast.21, f32[]{:T(128)} %constant.90.clone.1), kind=kCustom, calls=%fused_computation.58 | custom fusion | flops 1310720 | bytes 4194816 | tf_op jit(solution)/shard_map/scatter-add | solution.py:114
  (94 shorter events, 2.3 us)
Async XLA Ops:
  0.0 33.0 %copy-start = (bf16[4096,256]{1,0:T(8,128)(2,1)S(1)}, bf16[4096,256]{1,0:T(8,128)(2,1)}, u32[]{:S(2)}) copy-start(bf16[4096,256]{1,0:T(8,128)(2,1)} %param.14) | copy-start | bytes 6291460
  3.2 57.7 %copy-start.20 = (s32[2048,1]{0,1:T(1,128)}, s32[2048,1]{0,1:T(1,128)S(1)}, u32[]{:S(2)}) copy-start(s32[2048,1]{0,1:T(1,128)S(1)} %compare_select_fusion.5) | copy-start | bytes 24580
  32.3 0.6 copy-start.12
  54.2 6.0 %copy-start.21 = (f32[1,1024]{1,0:T(1,128)S(1)}, f32[1,1024]{1,0:T(1,128)}, u32[]{:S(2)}) copy-start(f32[1,1024]{1,0:T(1,128)} %param.13) | copy-start | bytes 12292
  54.2 41.3 %all-to-all-start.1 = ((bf16[128,40,256]{2,1,0:T(8,128)(2,1)}), bf16[128,40,256]{2,1,0:T(8,128)(2,1)}, u32[]{:S(2)}, u32[]{:S(2)}) async-start(bf16[128,40,256]{2,1,0:T(8,128)(2,1)} %bitcast.165), calls=%async_computation.1 | async-start | bytes 5242880 | tf_op jit(solution)/shard_map/all_to_all | solution.py:93
  95.5 9.6 %copy-start.15 = (bf16[256,256]{1,0:T(8,128)(2,1)S(1)}, bf16[256,256]{1,0:T(8,128)(2,1)}, u32[]{:S(2)}) copy-start(bf16[256,256]{1,0:T(8,128)(2,1)} %param.17) | copy-start | bytes 393220
  95.5 12.8 %copy-start.14 = (bf16[256,256]{1,0:T(8,128)(2,1)S(1)}, bf16[256,256]{1,0:T(8,128)(2,1)}, u32[]{:S(2)}) copy-start(bf16[256,256]{1,0:T(8,128)(2,1)} %param.16) | copy-start | bytes 393220
  104.3 8.4 %copy-start.9 = (bf16[256,256]{1,0:T(8,128)(2,1)S(1)}, bf16[256,256]{1,0:T(8,128)(2,1)}, u32[]{:S(2)}) copy-start(bf16[256,256]{1,0:T(8,128)(2,1)} %param.15) | copy-start | bytes 393220
  112.7 0.8 copy-start.7
  112.7 2.4 copy-start.18
  113.3 5.4 %copy-start.16 = (pred[1024]{0:T(1024)(128)(4,1)}, pred[1024]{0:T(1024)(128)(4,1)S(1)}, u32[]{:S(2)}) copy-start(pred[1024]{0:T(1024)(128)(4,1)S(1)} %iota_compare_fusion.5) | copy-start | bytes 3076 | tf_op jit(solution)/shard_map/while/body/eval_jaxpr/while
  118.1 3.2 %copy-start.1 = (f32[4,512,1024]{2,1,0:T(8,128)}, f32[4,512,1024]{2,1,0:T(8,128)S(1)}, u32[]{:S(2)}) copy-start(f32[4,512,1024]{2,1,0:T(8,128)S(1)} %get-tuple-element.254) | copy-start | bytes 25165828 | tf_op jit(solution)/shard_map/while/body/eval_jaxpr/while
  127.6 6.1 %copy-start.17 = (pred[1024]{0:T(1024)(128)(4,1)S(1)}, pred[1024]{0:T(1024)(128)(4,1)}, u32[]{:S(2)}) copy-start(pred[1024]{0:T(1024)(128)(4,1)} %copy-done.16) | copy-start | bytes 3076 | tf_op jit(solution)/shard_map/while/body/eval_jaxpr/while
  133.7 5.2 %copy-start.8 = (bf16[1024,256]{0,1:T(8,128)(2,1)S(1)}, bf16[1024,256]{0,1:T(8,128)(2,1)}, u32[]{:S(2)}) copy-start(bf16[1024,256]{0,1:T(8,128)(2,1)} %copy-done.7) | copy-start | bytes 1572868 | tf_op jit(solution)/shard_map/while/body/eval_jaxpr/while
  138.9 2.3 copy-start.2
  138.9 2.3 copy-start.3
  138.9 2.3 copy-start.5
  140.3 1.6 copy-start.10
  141.2 3.0 %copy-start.19 = (f32[2,512]{1,0:T(2,128)S(1)}, f32[2,512]{1,0:T(2,128)}, u32[]{:S(2)}) copy-start(f32[2,512]{1,0:T(2,128)} %copy-done.18) | copy-start | bytes 12292 | tf_op jit(solution)/shard_map/while/body/eval_jaxpr/while
  141.9 1.0 copy-start.4
  141.9 1.4 copy-start.6
  143.3 1.0 copy-start.11
  144.2 0.8 copy-start.7
  144.2 2.4 copy-start.18
  144.9 5.4 %copy-start.16 = (pred[1024]{0:T(1024)(128)(4,1)}, pred[1024]{0:T(1024)(128)(4,1)S(1)}, u32[]{:S(2)}) copy-start(pred[1024]{0:T(1024)(128)(4,1)S(1)} %iota_compare_fusion.5) | copy-start | bytes 3076 | tf_op jit(solution)/shard_map/while/body/eval_jaxpr/while
  149.6 3.2 %copy-start.1 = (f32[4,512,1024]{2,1,0:T(8,128)}, f32[4,512,1024]{2,1,0:T(8,128)S(1)}, u32[]{:S(2)}) copy-start(f32[4,512,1024]{2,1,0:T(8,128)S(1)} %get-tuple-element.254) | copy-start | bytes 25165828 | tf_op jit(solution)/shard_map/while/body/eval_jaxpr/while
  159.2 6.1 %copy-start.17 = (pred[1024]{0:T(1024)(128)(4,1)S(1)}, pred[1024]{0:T(1024)(128)(4,1)}, u32[]{:S(2)}) copy-start(pred[1024]{0:T(1024)(128)(4,1)} %copy-done.16) | copy-start | bytes 3076 | tf_op jit(solution)/shard_map/while/body/eval_jaxpr/while
  165.3 5.2 %copy-start.8 = (bf16[1024,256]{0,1:T(8,128)(2,1)S(1)}, bf16[1024,256]{0,1:T(8,128)(2,1)}, u32[]{:S(2)}) copy-start(bf16[1024,256]{0,1:T(8,128)(2,1)} %copy-done.7) | copy-start | bytes 1572868 | tf_op jit(solution)/shard_map/while/body/eval_jaxpr/while
  170.4 2.3 copy-start.2
  170.4 2.3 copy-start.3
  170.4 2.3 copy-start.5
  171.8 1.6 copy-start.10
  172.7 3.0 %copy-start.19 = (f32[2,512]{1,0:T(2,128)S(1)}, f32[2,512]{1,0:T(2,128)}, u32[]{:S(2)}) copy-start(f32[2,512]{1,0:T(2,128)} %copy-done.18) | copy-start | bytes 12292 | tf_op jit(solution)/shard_map/while/body/eval_jaxpr/while
  173.4 1.0 copy-start.4
  173.4 1.4 copy-start.6
  174.8 1.0 copy-start.11
  191.4 6.2 %copy-start.13 = (s32[128,1,40]{2,1,0:T(1,128)S(1)}, s32[128,1,40]{2,1,0:T(1,128)}, u32[]{:S(2)}) copy-start(s32[128,1,40]{2,1,0:T(1,128)} %copy-done.12) | copy-start | bytes 61444
  191.4 69.9 %all-to-all-start.2 = ((f32[128,40,256]{2,1,0:T(8,128)}), f32[128,40,256]{2,1,0:T(8,128)}, u32[]{:S(2)}, u32[]{:S(2)}) async-start(f32[128,40,256]{2,1,0:T(8,128)} %bitcast.162), calls=%async_computation.2 | async-start | bytes 10485760 | tf_op jit(solution)/shard_map/all_to_all | solution.py:106
where the time goes:
time: 295 us; the launch traced here: 294 us
  waiting for transfers between devices  97.4 us (33%)
  other arithmetic  68.3 us (23%)
  local copies, waits for them, and re-layouts  57 us (19%)
  matrix products  39.1 us (13%)
  blocking collectives  20.9 us (7%)
  starting transfers between devices  11 us (4%)
    all_to_all x1, waiting for transfers between devices, body(): lax.all_to_all(outgoing.reshape(devices, capacity, width), ('user', 'item...  62.8 us
    all_to_all x1, waiting for transfers between devices, body(): lax.all_to_all(found, ('user', 'item'), split_axis=0, concat_axis=0, tile...  34.6 us
    scatter-add x1, other arithmetic, body(): return grad_table.at[asked.reshape(-1)].add(arrived.reshape(-1, width))  33.1 us
    dot_general x6, matrix products, block_loss(): jnp.einsum('hjt,thd->jhd', attn, v_heads, preferred_element_type=jnp.floa...  22.2 us
    gather x1, local copies, waits for them, and re-layouts, body(): found = table[asked]  21.1 us
    all_to_all x1, blocking collectives, body(): lax.all_to_all(request.reshape(devices, capacity), ('user', 'item'), spli...  20.9 us
    scatter x1, other arithmetic, body(): jnp.zeros((devices * capacity, width), jnp.float32).at[place].set(grad_flat)  12.5 us
    dot_general x6, matrix products, block_loss(): jnp.einsum('jhd,thd->hjt', q_heads, k_heads, preferred_element_type=jnp.f...  10.4 us
  transfers between devices with their start and end apart: 2, of which 2 were waited for; matrix products, arithmetic and copies ran while one was open for 1% of the time, Pallas kernels for 0%

commit v1 on v0

v1 whole, which is shorter than its diff:
```python
import math

import jax
import jax.numpy as jnp
from jax import lax
from jax.experimental import pallas as pl
from jax.experimental.pallas import tpu as pltpu
from jax.sharding import PartitionSpec as P

HEADS = 4
GRAD_SCALE = 1024


CAND = 1024
HIST = 1024
WIDTH = 256
HEAD = 64
BLOCK = 256


def dot(a, b):
    return jnp.dot(a, b, preferred_element_type=jnp.float32)


def dot_tn(a, b):
    return lax.dot_general(a, b, (((0,), (0,)), ((), ())), preferred_element_type=jnp.float32)


def dot_nt(a, b):
    return lax.dot_general(a, b, (((1,), (1,)), ((), ())), preferred_element_type=jnp.float32)


def attention_kernel(len_ref, rows_ref, teacher_ref, wq_ref, wk_ref, wv_ref, out_ref, q_s, kt_s, vt_s, vk1_s, cq_s, ee_s, xx_s, dvk_s):
    half = jnp.bfloat16
    length = len_ref[0]
    live = lax.broadcasted_iota(jnp.int32, (HIST, 128), 0) < length
    live2 = jnp.concatenate([live, live], axis=1)
    hist = jnp.where(live2, rows_ref[CAND:, :], jnp.zeros((), half))
    keys = dot(hist, wk_ref[...]).astype(half)
    values = dot(hist, wv_ref[...]).astype(half)
    kt_s[...] = keys.T
    vt_s[...] = values.T
    cand = rows_ref[:CAND, :]
    query = dot(cand, wq_ref[...]).astype(half)
    q_s[...] = query
    ones = jnp.where(live, 1.0, 0.0).astype(half)
    for h in range(HEADS):
        part = slice(h * HEAD, (h + 1) * HEAD)
        vk1_s[h] = jnp.concatenate([values[:, part], keys[:, part], ones], axis=1)
        cq_s[h] = jnp.concatenate([cand[:, part], query[:, part]], axis=1)
    dvk_s[...] = jnp.zeros_like(dvk_s)
    first = lax.broadcasted_iota(jnp.int32, (BLOCK, 128), 1) < HEAD
    scale = 1.0 / (math.sqrt(HEAD) * math.log(2.0))

    def step(jb, carry):
        here = pl.ds(pl.multiple_of(jb * BLOCK, BLOCK), BLOCK)
        logit = jnp.zeros((BLOCK, 128), jnp.float32)
        kept = []
        for h in range(HEADS):
            part = slice(h * HEAD, (h + 1) * HEAD)
            cq = cq_s[h, here, :]
            score = dot(cq[:, HEAD:], kt_s[part, :])
            worth = dot(cq[:, :HEAD], vt_s[part, :])
            top = jnp.max(score, axis=1, keepdims=True)
            raised = jnp.exp2((score - top) * scale)
            ee_s[h, :BLOCK, :] = raised.astype(half)
            ee_s[h, BLOCK:, :] = (raised * worth).astype(half)
            both = dot(ee_s[h], vk1_s[h])
            inverse = 1.0 / both[:BLOCK, 128:]
            mean = both[BLOCK:, 128:] * inverse
            plain = both[:BLOCK, :128] * inverse
            lifted = both[BLOCK:, :128] * inverse - mean * plain
            logit = logit + mean
            kept.append((inverse, mean, plain, lifted))
        logit = logit / math.sqrt(WIDTH)
        factor = (GRAD_SCALE / math.sqrt(WIDTH)) * (jax.nn.sigmoid(logit) - jax.nn.sigmoid(teacher_ref[here, :]))
        direct, turned = [], []
        for h in range(HEADS):
            inverse, mean, plain, lifted = kept[h]
            cq = cq_s[h, here, :].astype(jnp.float32)
            weight = factor * inverse
            eighth = weight * (1.0 / math.sqrt(HEAD))
            xx_s[h, :BLOCK, :] = (cq * jnp.where(first, weight, -mean * eighth)).astype(half)
            xx_s[h, BLOCK:, :] = (cq * jnp.where(first, 0.0, eighth)).astype(half)
            dvk_s[h] += dot_tn(xx_s[h], ee_s[h])
            direct.append(plain[:, :HEAD] * factor[:, :HEAD])
            turned.append((lifted[:, HEAD:] * (factor[:, HEAD:] * (1.0 / math.sqrt(HEAD)))))
        back = jnp.concatenate(turned, axis=1).astype(half)
        grad = jnp.concatenate(direct, axis=1) + dot_nt(back, wq_ref[...])
        out_ref[here, :] = grad.astype(half)
        return carry

    lax.fori_loop(0, CAND // BLOCK, step, 0)
    dv = jnp.concatenate([dvk_s[h, :HEAD, :] for h in range(HEADS)], axis=0).astype(half)
    dk = jnp.concatenate([dvk_s[h, HEAD:, :] for h in range(HEADS)], axis=0).astype(half)
    grad_hist = dot_nt(dv.T, wv_ref[...]) + dot_nt(dk.T, wk_ref[...])
    out_ref[CAND:, :] = jnp.where(live2, grad_hist, 0.0).astype(half)


def attention(rows, length, teacher, w_query, w_key, w_value):
    half = jnp.bfloat16
    space = pl.BlockSpec(memory_space=pltpu.VMEM)
    return pl.pallas_call(
        attention_kernel,
        out_shape=jax.ShapeDtypeStruct((CAND + HIST, WIDTH), half),
        in_specs=[pl.BlockSpec(memory_space=pltpu.SMEM)] + [space] * 5,
        out_specs=space,
        scratch_shapes=[
            pltpu.VMEM((CAND, WIDTH), half),
            pltpu.VMEM((WIDTH, HIST), half),
            pltpu.VMEM((WIDTH, HIST), half),
            pltpu.VMEM((HEADS, HIST, 256), half),
            pltpu.VMEM((HEADS, CAND, 128), half),
            pltpu.VMEM((HEADS, 2 * BLOCK, HIST), half),
            pltpu.VMEM((HEADS, 2 * BLOCK, 128), half),
            pltpu.VMEM((HEADS, 128, HIST), jnp.float32),
        ],
        compiler_params=pltpu.CompilerParams(vmem_limit_bytes=48 * 2**20),
        cost_estimate=pl.CostEstimate(flops=4 * 10**9, bytes_accessed=3 * 2**20, transcendentals=4 * 2**20),
        name="attention",
    )(length, rows, jnp.broadcast_to(teacher.reshape(CAND, 1), (CAND, 128)), w_query, w_key, w_value)


def body(cand_ids, hist_ids, hist_len, teacher, table, w_query, w_key, w_value):
    rows_dev, width = table.shape
    users_here, cand = cand_ids.shape
    user_count = lax.axis_size("user")
    item_count = lax.axis_size("item")
    devices = user_count * item_count
    wanted = jnp.concatenate([cand_ids, hist_ids], axis=1).reshape(-1)
    slots = wanted.shape[0]
    capacity = 5 * (slots // devices) // 2
    owner = wanted // rows_dev
    local = wanted % rows_dev
    onehot = (owner[:, None] == jnp.arange(devices, dtype=jnp.int32)[None, :]).astype(jnp.int32)
    rank = jnp.sum(jnp.cumsum(onehot, axis=0) * onehot, axis=1) - 1
    place = owner * capacity + rank
    request = jnp.zeros((devices * capacity,), jnp.int32).at[place].set(local)
    asked = lax.all_to_all(
        request.reshape(devices, capacity),
        ("user", "item"),
        split_axis=0,
        concat_axis=0,
        tiled=True,
    )
    found = table[asked]
    asked, fetched = (
        asked,
        lax.all_to_all(found, ("user", "item"), split_axis=0, concat_axis=0, tiled=True),
    )
    rows = fetched.reshape(devices * capacity, width)[place].reshape(users_here, -1, width)
    grad_flat = attention(rows.reshape(-1, width), hist_len, teacher, w_query, w_key, w_value)
    outgoing = jnp.zeros((devices * capacity, width), jnp.bfloat16).at[place].set(grad_flat)
    arrived = lax.all_to_all(
        outgoing.reshape(devices, capacity, width),
        ("user", "item"),
        split_axis=0,
        concat_axis=0,
        tiled=True,
    )
    grad_table = jnp.zeros((rows_dev, width), jnp.float32)
    return grad_table.at[asked.reshape(-1)].add(arrived.reshape(-1, width).astype(jnp.float32))


def solution(mesh):
    placed = (
        P(("user", "item"), None),
        P(("user", "item"), None),
        P(("user", "item")),
        P(("user", "item"), None),
        P(("user", "item"), None),
        P(),
        P(),
        P(),
    )
    return jax.shard_map(
        body, mesh=mesh, in_specs=placed, out_specs=P(("user", "item"), None), check_vma=False
    )
```

time: 295 us -> 210 us (0.71)
  matrix products: 39.1 us -> 0 us
  other arithmetic: 68.3 us -> 34 us
  waiting for transfers between devices: 97.4 us -> 69.6 us
  Pallas kernels: 0 us -> 18 us
    dot_general x20 -> x0, matrix products: 39.1 us -> none  [the longest x6 22.2 us: block_loss(): jnp.einsum('hjt,thd->jhd', attn, v_heads, preferred_element_type=jnp.floa...]
    all_to_all x1, waiting for transfers between devices: 62.8 us -> 34.4 us  [body(): lax.all_to_all(outgoing.reshape(devices, capacity, width), ('user', 'item...]
    pallas_call x0 -> x1, Pallas kernels: none -> 18 us  [attention(): pl.pallas_call(attention_kernel, out_shape=jax.ShapeDtypeStruct((CAND + H...]
    scatter x1 -> x0, other arithmetic: 12.5 us -> none  [body(): jnp.zeros((devices * capacity, width), jnp.float32).at[place].set(grad_flat)]
    div x6 -> x0, other arithmetic: 11.6 us -> none  [the longest x2 10.3 us: block_loss(): score = score / math.sqrt(q_heads.shape[2])]
    scatter x0 -> x1, local copies, waits for them, and re-layouts: none -> 11.5 us  [body(): jnp.zeros((devices * capacity, width), jnp.bfloat16).at[place]]
    while x56 -> x0, local copies, waits for them, and re-layouts: 5.89 us -> none
    convert_element_type x3 -> x0, other arithmetic: 5.74 us -> none  [the longest x2 3.65 us: block_loss(): (raised / jnp.sum(raised, axis=2, keepdims=True)).astype(jnp.bfloat16)]
where the time goes in v1:
time: 210 us; the launch traced here: 209 us
  waiting for transfers between devices  69.6 us (33%)
  local copies, waits for them, and re-layouts  54.8 us (26%)
  other arithmetic  34 us (16%)
  blocking collectives  20.9 us (10%)
  Pallas kernels  18 us (9%)
  starting transfers between devices  10.8 us (5%)
    all_to_all x1, waiting for transfers between devices, body(): lax.all_to_all(found, ('user', 'item'), split_axis=0, concat_axis=0, tile...  35.3 us
    all_to_all x1, waiting for transfers between devices, body(): lax.all_to_all(outgoing.reshape(devices, capacity, width), ('user', 'item...  34.4 us
    scatter-add x1, other arithmetic, body(): grad_table.at[asked.reshape(-1)]  32 us
    gather x1, local copies, waits for them, and re-layouts, body(): found = table[asked]  21.1 us
    all_to_all x1, blocking collectives, body(): lax.all_to_all(request.reshape(devices, capacity), ('user', 'item'), spli...  20.9 us
    pallas_call x1, Pallas kernels, attention(): pl.pallas_call(attention_kernel, out_shape=jax.ShapeDtypeStruct((CAND + H...  18 us
    scatter x1, local copies, waits for them, and re-layouts, body(): jnp.zeros((devices * capacity, width), jnp.bfloat16).at[place]  11.5 us
    gather x1, local copies, waits for them, and re-layouts, body(): fetched.reshape(devices * capacity, width)[place]  8.76 us
  transfers between devices with their start and end apart: 2, of which 2 were waited for; matrix products, arithmetic and copies ran while one was open for 1% of the time, Pallas kernels for 0%

profile of v1, /device:TPU:1, one launch (start us, length us, event | category | flops | bytes accessed | tf_op | source)
XLA Modules:
  0.0 209.1 jit_solution(1491144347183951061)
XLA Ops:
  0.0 0.0 copy-start
  0.0 0.8 constant_dynamic-update-slice_fusion.1
  0.8 0.7 constant_dynamic-update-slice_fusion
  1.6 0.1 copy.12
  1.7 0.3 fusion.6
  2.1 0.1 broadcast_add_fusion
  2.1 0.3 copy.13
  2.5 0.6 fusion.5
  3.1 0.1 compare_select_fusion.2
  3.2 8.1 %scatter_custom_fusion = s32[5120]{0:T(1024)S(1)} fusion(s32[2048]{0:T(1024)S(1)} %bitcast.41, s32[2048]{0:T(1024)S(1)} %get-tuple-element.5, s32[]{:T(128)} %constant.39.clone.1), kind=kCustom, calls=%fused_computation.35 | custom fusion | bytes 20484 | tf_op jit(solution)/shard_map/scatter | solution.py:138
  11.3 0.1 all_to_all.14
  11.4 20.9 %all_to_all.22 = s32[128,1,40]{2,1,0:T(1,128)S(1)} all-to-all(s32[128,1,40]{2,1,0:T(1,128)S(1)} %bitcast.38), channel_id=1, replica_groups=mesh['user'=16,'item'=8] {'user','item'}, dimensions={0} | all-to-all | bytes 40960 | tf_op jit(solution)/shard_map/all_to_all | solution.py:139
  32.3 0.0 copy-start.5
  32.3 0.6 copy-done.5
  32.9 0.1 reshape.215
  33.0 0.0 copy-done
  33.0 21.1 %gather_fusion = bf16[5120,256]{1,0:T(8,128)(2,1)} fusion(bf16[4096,256]{1,0:T(8,128)(2,1)S(1)} %copy-done, s32[5120]{0:T(1024)S(1)} %broadcast_clamp_fusion), kind=kCustom, calls=%fused_computation | custom fusion | bytes 5263360 | tf_op jit(solution)/shard_map/gather | solution.py:146
  54.1 5.2 %all-to-all-start.1 = ((bf16[128,40,256]{2,1,0:T(8,128)(2,1)}), bf16[128,40,256]{2,1,0:T(8,128)(2,1)}, u32[]{:S(2)}, u32[]{:S(2)}) async-start(bf16[128,40,256]{2,1,0:T(8,128)(2,1)} %bitcast.36), calls=%async_computation.1 | async-start | bytes 5242880 | tf_op jit(solution)/shard_map/all_to_all | solution.py:149
  60.0 35.3 %all-to-all-done.1 = bf16[128,40,256]{2,1,0:T(8,128)(2,1)} async-done(((bf16[128,40,256]{2,1,0:T(8,128)(2,1)}), bf16[128,40,256]{2,1,0:T(8,128)(2,1)}, u32[]{:S(2)}, u32[]{:S(2)}) %all-to-all-start.1) | async-done | bytes 2621472 | tf_op jit(solution)/shard_map/all_to_all | solution.py:149
  95.3 0.0 copy-start.2
  95.3 0.0 copy-start.3
  95.3 0.0 copy-start.4
  95.3 8.8 %gather_fusion.1 = bf16[2048,256]{1,0:T(8,128)(2,1)S(1)} fusion(bf16[5120,256]{1,0:T(8,128)(2,1)} %bitcast.12, s32[2048]{0:T(1024)S(1)} %broadcast_clamp_fusion.1), kind=kCustom, calls=%fused_computation.1 | custom fusion | bytes 2105344 | tf_op jit(solution)/shard_map/gather | solution.py:151
  104.1 0.9 broadcast_in_dim.11.teacher_ref
  105.0 0.0 copy-done.2
  105.0 0.0 copy-done.3
  105.0 0.0 copy-done.4
  105.0 18.0 %attention.1 = bf16[2048,256]{1,0:T(8,128)(2,1)S(1)} custom-call(s32[1]{0:T(128)S(6)} %copy.16.len_ref, bf16[2048,256]{1,0:T(8,128)(2,1)S(1)} %gather_fusion.1, f32[1024,128]{1,0:T(8,128)S(1)} %broadcast_in_dim.11.teacher_ref, bf16[256,256]{1,0:T(8,128)(2,1)S(1)} %copy-done.2, bf16[256,256]{1,0:T(8,128)(2,1)S(1)} %copy-done.3, bf16[256,256]{1,0:T(8,128)(2,1)S(1)} %copy-done.4), custom_call_target="tpu_custom_call" | custom-call | flops 4000000000 | bytes 3145728 | tf_op jit(solution)/shard_map/attention/pallas_call | solution.py:103
  123.1 0.0 copy-start.1
  123.1 1.0 copy-done.1
  124.0 11.5 %scatter_custom_fusion.1 = bf16[5120,256]{1,0:T(8,128)(2,1)} fusion(s32[2048]{0:T(1024)S(1)} %bitcast.43, bf16[2048,256]{1,0:T(8,128)(2,1)} %copy-done.1, bf16[]{:T(256)} %constant.47.clone.1), kind=kCustom, calls=%fused_computation.8 | custom fusion | bytes 2621952 | tf_op jit(solution)/shard_map/scatter | solution.py:153
  135.6 0.0 copy-start.6
  135.6 5.6 %all-to-all-start.2 = ((bf16[128,40,256]{2,1,0:T(8,128)(2,1)}), bf16[128,40,256]{2,1,0:T(8,128)(2,1)}, u32[]{:S(2)}, u32[]{:S(2)}) async-start(bf16[128,40,256]{2,1,0:T(8,128)(2,1)} %bitcast.35), calls=%async_computation.2 | async-start | bytes 5242880 | tf_op jit(solution)/shard_map/all_to_all | solution.py:154
  141.2 0.6 broadcast.207
  141.8 0.0 copy-done.6
  141.8 0.9 reduce.3
  142.6 0.1 reshape.209
  142.8 34.4 %all-to-all-done.2 = bf16[128,40,256]{2,1,0:T(8,128)(2,1)} async-done(((bf16[128,40,256]{2,1,0:T(8,128)(2,1)}), bf16[128,40,256]{2,1,0:T(8,128)(2,1)}, u32[]{:S(2)}, u32[]{:S(2)}) %all-to-all-start.2) | async-done | bytes 2621472 | tf_op jit(solution)/shard_map/all_to_all | solution.py:154
  177.1 32.0 %scatter_custom_fusion.2 = f32[4096,256]{1,0:T(8,128)} fusion(s32[5120]{0:T(1024)S(1)} %bitcast.45, bf16[5120,256]{1,0:T(8,128)(2,1)} %bitcast.17, f32[]{:T(128)} %constant.38.clone.1), kind=kCustom, calls=%fused_computation.5 | custom fusion | flops 2621440 | bytes 6815748 | tf_op jit(solution)/shard_map/scatter-add | solution.py:162
  (10 shorter events, 0.1 us)
Async XLA Ops:
  0.0 33.0 %copy-start = (bf16[4096,256]{1,0:T(8,128)(2,1)S(1)}, bf16[4096,256]{1,0:T(8,128)(2,1)}, u32[]{:S(2)}) copy-start(bf16[4096,256]{1,0:T(8,128)(2,1)} %param.12) | copy-start | bytes 6291460
  32.3 0.6 copy-start.5
  54.1 41.2 %all-to-all-start.1 = ((bf16[128,40,256]{2,1,0:T(8,128)(2,1)}), bf16[128,40,256]{2,1,0:T(8,128)(2,1)}, u32[]{:S(2)}, u32[]{:S(2)}) async-start(bf16[128,40,256]{2,1,0:T(8,128)(2,1)} %bitcast.36), calls=%async_computation.1 | async-start | bytes 5242880 | tf_op jit(solution)/shard_map/all_to_all | solution.py:149
  95.3 9.7 %copy-start.2 = (bf16[256,256]{1,0:T(8,128)(2,1)S(1)}, bf16[256,256]{1,0:T(8,128)(2,1)}, u32[]{:S(2)}) copy-start(bf16[256,256]{1,0:T(8,128)(2,1)} %wq_ref.1) | copy-start | bytes 393220
  95.3 9.7 %copy-start.3 = (bf16[256,256]{1,0:T(8,128)(2,1)S(1)}, bf16[256,256]{1,0:T(8,128)(2,1)}, u32[]{:S(2)}) copy-start(bf16[256,256]{1,0:T(8,128)(2,1)} %wk_ref.1) | copy-start | bytes 393220
  95.3 9.7 %copy-start.4 = (bf16[256,256]{1,0:T(8,128)(2,1)S(1)}, bf16[256,256]{1,0:T(8,128)(2,1)}, u32[]{:S(2)}) copy-start(bf16[256,256]{1,0:T(8,128)(2,1)} %wv_ref.1) | copy-start | bytes 393220
  123.1 1.0 copy-start.1
  135.6 6.2 %copy-start.6 = (s32[128,1,40]{2,1,0:T(1,128)S(1)}, s32[128,1,40]{2,1,0:T(1,128)}, u32[]{:S(2)}) copy-start(s32[128,1,40]{2,1,0:T(1,128)} %copy-done.5) | copy-start | bytes 61444
  135.6 41.5 %all-to-all-start.2 = ((bf16[128,40,256]{2,1,0:T(8,128)(2,1)}), bf16[128,40,256]{2,1,0:T(8,128)(2,1)}, u32[]{:S(2)}, u32[]{:S(2)}) async-start(bf16[128,40,256]{2,1,0:T(8,128)(2,1)} %bitcast.35), calls=%async_computation.2 | async-start | bytes 5242880 | tf_op jit(solution)/shard_map/all_to_all | solution.py:154

commit v2 on v1

--- a/solution.py
+++ b/solution.py
@@ -121,45 +121,281 @@
     )(length, rows, jnp.broadcast_to(teacher.reshape(CAND, 1), (CAND, 128)), w_query, w_key, w_value)
 
 
+USERS = 16
+ITEMS = 8
+PEERS = USERS * ITEMS
+CAP = 40
+TABLE_ROWS = 4096
+GROUP = 8
+SLOTS = GROUP * CAP
+GROUPS = PEERS // GROUP
+ROWS = CAND + HIST
+MESH = pl.DeviceIdType.MESH
+
+
+def partner(k, sign):
+    dz = k % 4
+    dx = (k // 4 + dz) % 4
+    dy = (k // 16 + dz) % 4
+    dc = k // 64
+    user = lax.axis_index("user")
+    item = lax.axis_index("item")
+    z = (user // 4 + 4 + sign * dz) % 4
+    x = (user % 4 + 4 + sign * dx) % 4
+    y = (item // 2 + 4 + sign * dy) % 4
+    c = (item % 2 + dc) % 2
+    return z * 4 + x, y * 2 + c
+
+
+def linear(where):
+    return where[0] * ITEMS + where[1]
+
+
+def one_hot(match):
+    return jnp.where(match, 1.0, 0.0).astype(jnp.bfloat16)
+
+
+def greet():
+    user = lax.axis_index("user")
+    item = lax.axis_index("item")
+    barrier = pltpu.get_barrier_semaphore()
+    for step in range(1, ITEMS):
+        pl.semaphore_signal(barrier, inc=1, device_id=(user, (item + step) % ITEMS), device_id_type=MESH)
+    for step in range(1, USERS):
+        pl.semaphore_signal(barrier, inc=1, device_id=((user + step) % USERS, item), device_id_type=MESH)
+    return barrier
+
+
+def requests(cand_ref, hist_ref, place_ref):
+    half = jnp.bfloat16
+    rows = lax.broadcasted_iota(jnp.int32, (PEERS, 256), 0)
+    slot = lax.broadcasted_iota(jnp.int32, (64, 256), 0).astype(jnp.float32)
+    upper = one_hot(lax.broadcasted_iota(jnp.int32, (256, 256), 0) < lax.broadcasted_iota(jnp.int32, (256, 256), 1))
+    taken = jnp.zeros((PEERS, 1), jnp.float32)
+    wanted = jnp.zeros((PEERS, 128), jnp.float32)
+    for c in range(ROWS // 256):
+        at = c * 256
+        ids = cand_ref[:, at:at + 256] if at < CAND else hist_ref[:, at - CAND:at - CAND + 256]
+        owner = ids // TABLE_ROWS
+        local = ids % TABLE_ROWS
+        full = jnp.where(rows == owner, 1.0, 0.0)
+        chosen = full.astype(half)
+        rank = jnp.sum(full * (dot(chosen, upper) + taken), axis=0, keepdims=True)
+        taken = taken + jnp.sum(full, axis=1, keepdims=True)
+        place_ref[:, at:at + 256] = owner.astype(jnp.float32) * CAP + rank
+        mine = slot == rank
+        high = (local // 64).astype(jnp.float32)
+        low = (local % 64).astype(jnp.float32)
+        split = jnp.concatenate([jnp.where(mine, high, 0.0), jnp.where(mine, low, 0.0)], axis=0).astype(half)
+        wanted = wanted + dot_nt(chosen, split)
+    return jnp.concatenate([wanted[:, :64] * 64.0 + wanted[:, 64:], jnp.zeros((PEERS, 64), jnp.float32)], axis=1)
+
+
+def fetch_kernel(cand_ref, hist_ref, table_ref, rows_ref, place_ref, asked_ref, want_s, item_out, item_in, user_out, wide_s, send_s, recv_s, pos_s, acc_s, isend, irecv, usend, urecv, rsend, rrecv):
+    half = jnp.bfloat16
+    user = lax.axis_index("user")
+    item = lax.axis_index("item")
+    barrier = greet()
+    want_s[...] = requests(cand_ref, hist_ref, place_ref)
+    for i in range(ITEMS):
+        item_out[i] = want_s[pl.ds(i, USERS, stride=ITEMS), :]
+    pl.semaphore_wait(barrier, USERS + ITEMS - 2)
+    for step in range(1, ITEMS):
+        to = (item + step) % ITEMS
+        pltpu.make_async_remote_copy(
+            src_ref=item_out.at[to], dst_ref=item_in.at[item], send_sem=isend, recv_sem=irecv,
+            device_id=(user, to), device_id_type=MESH).start()
+    item_in[item] = item_out[item]
+    pos_s[...] = jnp.broadcast_to(place_ref[...], (128, ROWS)).T
+    acc_s[...] = jnp.zeros_like(acc_s)
+    pltpu.make_async_copy(item_out.at[pl.ds(1, ITEMS - 1)], item_in.at[pl.ds(1, ITEMS - 1)], irecv).wait()
+    for u in range(USERS):
+        user_out[u] = jnp.concatenate([item_in[i, u:u + 1, :] for i in range(ITEMS)], axis=0)
+    for step in range(1, USERS):
+        to = (user + step) % USERS
+        pltpu.make_async_remote_copy(
+            src_ref=user_out.at[to], dst_ref=asked_ref.at[user], send_sem=usend, recv_sem=urecv,
+            device_id=(to, item), device_id_type=MESH).start()
+    asked_ref[user] = user_out[user]
+    pltpu.make_async_copy(user_out.at[pl.ds(1, USERS - 1)], asked_ref.at[pl.ds(1, USERS - 1)], urecv).wait()
+    turned = asked_ref[...].reshape(PEERS, 128).T
+    for p in range(PEERS):
+        wide_s[p] = jnp.broadcast_to(turned[:CAP, p:p + 1], (CAP, 128))
+    lane = lax.broadcasted_iota(jnp.int32, (SLOTS, 256), 1).astype(jnp.float32)
+
+    def give(n, carry):
+        wide = jnp.concatenate([wide_s[linear(partner(n * GROUP + kk, 1))] for kk in range(GROUP)], axis=0)
+        ids = jnp.concatenate([wide, wide], axis=1)
+        found = jnp.zeros((SLOTS, WIDTH), jnp.float32)
+        for c in range(TABLE_ROWS // 256):
+            found = found + dot(one_hot(ids == lane + c * 256.0), table_ref[c * 256:(c + 1) * 256, :])
+        for kk in range(GROUP):
+            k = n * GROUP + kk
+            send_s[k] = found[kk * CAP:(kk + 1) * CAP].astype(half)
+
+            def start():
+                pltpu.make_async_remote_copy(
+                    src_ref=send_s.at[k], dst_ref=recv_s.at[k], send_sem=rsend, recv_sem=rrecv.at[n],
+                    device_id=partner(k, 1), device_id_type=MESH).start()
+
+            if kk == 0:
+                pl.when(n > 0)(start)
+            else:
+                start()
+        return carry
+
+    lax.fori_loop(0, GROUPS, give, 0)
+    recv_s[0] = send_s[0]
+    spot = lax.broadcasted_iota(jnp.int32, (8, SLOTS), 1)
+
+    def take(n, carry):
+        @pl.when(n == 0)
+        def _():
+            pltpu.make_async_copy(send_s.at[pl.ds(1, GROUP - 1)], recv_s.at[pl.ds(1, GROUP - 1)], rrecv.at[0]).wait()
+
+        @pl.when(n > 0)
+        def _():
+            here = pl.ds(n * GROUP, GROUP)
+            pltpu.make_async_copy(send_s.at[here], recv_s.at[here], rrecv.at[n]).wait()
+
+        slab = recv_s[pl.ds(n * GROUP, GROUP)].astype(jnp.float32).reshape(SLOTS, WIDTH).astype(half)
+        slots = jnp.zeros((8, SLOTS), jnp.int32)
+        for kk in range(GROUP):
+            base = (linear(partner(n * GROUP + kk, -1)) - kk) * CAP
+            slots = jnp.where(spot >= kk * CAP, spot + base, slots)
+        slots = slots[:1].astype(jnp.float32)
+        for r in range(ROWS // 512):
+            at = slice(r * 512, (r + 1) * 512)
+            pos = pos_s[at, :]
+            pos = jnp.concatenate([pos, pos, pos[:, :SLOTS - 256]], axis=1)
+            acc_s[at, :] += dot(one_hot(pos == slots), slab)
+        return carry
+
+    lax.fori_loop(0, GROUPS, take, 0)
+    rows_ref[...] = acc_s[...].astype(half)
+    pltpu.make_async_copy(item_out.at[pl.ds(1, ITEMS - 1)], item_in.at[pl.ds(1, ITEMS - 1)], isend).wait()
+    pltpu.make_async_copy(user_out.at[pl.ds(1, USERS - 1)], asked_ref.at[pl.ds(1, USERS - 1)], usend).wait()
+    pltpu.make_async_copy(send_s.at[pl.ds(1, PEERS - 1)], recv_s.at[pl.ds(1, PEERS - 1)], rsend).wait()
+
+
+def fetch(cand_ids, hist_ids, table):
+    half = jnp.bfloat16
+    space = pl.BlockSpec(memory_space=pltpu.VMEM)
+    sem = pltpu.SemaphoreType.DMA
+    return pl.pallas_call(
+        fetch_kernel,
+        out_shape=[
+            jax.ShapeDtypeStruct((ROWS, WIDTH), half),
+            jax.ShapeDtypeStruct((1, ROWS), jnp.float32),
+            jax.ShapeDtypeStruct((USERS, ITEMS, 128), jnp.float32),
+        ],
+        in_specs=[space] * 3,
+        out_specs=[space] * 3,
+        scratch_shapes=[
+            pltpu.VMEM((PEERS, 128), jnp.float32),
+            pltpu.VMEM((ITEMS, USERS, 128), jnp.float32),
+            pltpu.VMEM((ITEMS, USERS, 128), jnp.float32),
+            pltpu.VMEM((USERS, ITEMS, 128), jnp.float32),
+            pltpu.VMEM((PEERS, CAP, 128), jnp.float32),
+            pltpu.VMEM((PEERS, CAP, WIDTH), half),
+            pltpu.VMEM((PEERS, CAP, WIDTH), half),
+            pltpu.VMEM((ROWS, 128), jnp.float32),
+            pltpu.VMEM((ROWS, WIDTH), jnp.float32),
+            sem(()), sem(()), sem(()), sem(()), sem(()), sem((GROUPS,)),
+        ],
+        compiler_params=pltpu.CompilerParams(collective_id=0, has_side_effects=True, vmem_limit_bytes=48 * 2**20),
+        name="fetch",
+    )(cand_ids, hist_ids, table)
+
+
+def give_back_kernel(grad_ref, place_ref, asked_ref, out_ref, send_s, recv_s, known, rsend, rrecv):
+    half = jnp.bfloat16
+    user = lax.axis_index("user")
+    item = lax.axis_index("item")
+    barrier = greet()
+    pl.semaphore_wait(barrier, USERS + ITEMS - 2)
+    for step in range(1, USERS):
+        pl.semaphore_signal(known, inc=1, device_id=((user + step) % USERS, item), device_id_type=MESH)
+    pl.semaphore_wait(known, USERS - 1)
+    deep = lax.broadcasted_iota(jnp.int32, (CAP, 128), 0)
+
+    def give(n, carry):
+        slots = jnp.concatenate([deep + linear(partner(n * GROUP + kk, 1)) * CAP for kk in range(GROUP)], axis=0)
+        slots = slots.astype(jnp.float32)
+        slots = jnp.concatenate([slots, slots], axis=1)
+        found = jnp.zeros((SLOTS, WIDTH), jnp.float32)
+        for c in range(ROWS // 256):
+            at = slice(c * 256, (c + 1) * 256)
+            found = found + dot(one_hot(slots == place_ref[:, at]), grad_ref[at, :])
+        for kk in range(GROUP):
+            k = n * GROUP + kk
+            send_s[k] = found[kk * CAP:(kk + 1) * CAP].astype(half)
+
+            def start():
+                pltpu.make_async_remote_copy(
+                    src_ref=send_s.at[k], dst_ref=recv_s.at[k], send_sem=rsend, recv_sem=rrecv.at[n],
+                    device_id=partner(k, 1), device_id_type=MESH).start()
+
+            if kk == 0:
+                pl.when(n > 0)(start)
+            else:
+                start()
+        return carry
+
+    lax.fori_loop(0, GROUPS, give, 0)
+    recv_s[0] = send_s[0]
+    out_ref[...] = jnp.zeros_like(out_ref)
+    high = lax.broadcasted_iota(jnp.int32, (512, SLOTS), 0).astype(jnp.float32)
+
+    def take(n, carry):
+        @pl.when(n == 0)
+        def _():
+            pltpu.make_async_copy(send_s.at[pl.ds(1, GROUP - 1)], recv_s.at[pl.ds(1, GROUP - 1)], rrecv.at[0]).wait()
+
+        @pl.when(n > 0)
+        def _():
+            here = pl.ds(n * GROUP, GROUP)
+            pltpu.make_async_copy(send_s.at[here], recv_s.at[here], rrecv.at[n]).wait()
+
+        slab = recv_s[pl.ds(n * GROUP, GROUP)].astype(jnp.float32).reshape(SLOTS, WIDTH).astype(half)
+        ids = []
+        for kk in range(GROUP):
+            source = partner(n * GROUP + kk, -1)
+            ids.append(asked_ref[source[0], pl.ds(source[1], 1), :][:, :CAP])
+        ids = jnp.concatenate(ids, axis=1)
+        for r in range(TABLE_ROWS // 512):
+            at = slice(r * 512, (r + 1) * 512)
+            out_ref[at, :] += dot(one_hot(high + r * 512.0 == ids), slab)
+        return carry
+
+    lax.fori_loop(0, GROUPS, take, 0)
+    pltpu.make_async_copy(send_s.at[pl.ds(1, PEERS - 1)], recv_s.at[pl.ds(1, PEERS - 1)], rsend).wait()
+
+
+def give_back(grads, place, asked):
+    half = jnp.bfloat16
+    space = pl.BlockSpec(memory_space=pltpu.VMEM)
+    sem = pltpu.SemaphoreType.DMA
+    return pl.pallas_call(
+        give_back_kernel,
+        out_shape=jax.ShapeDtypeStruct((TABLE_ROWS, WIDTH), jnp.float32),
+        in_specs=[space] * 3,
+        out_specs=space,
+        scratch_shapes=[
+            pltpu.VMEM((PEERS, CAP, WIDTH), half),
+            pltpu.VMEM((PEERS, CAP, WIDTH), half),
+            pltpu.SemaphoreType.REGULAR,
+            sem(()), sem((GROUPS,)),
+        ],
+        compiler_params=pltpu.CompilerParams(collective_id=1, has_side_effects=True, vmem_limit_bytes=48 * 2**20),
+        name="give_back",
+    )(grads, place, asked)
+
+
 def body(cand_ids, hist_ids, hist_len, teacher, table, w_query, w_key, w_value):
-    rows_dev, width = table.shape
-    users_here, cand = cand_ids.shape
-    user_count = lax.axis_size("user")
-    item_count = lax.axis_size("item")
-    devices = user_count * item_count
-    wanted = jnp.concatenate([cand_ids, hist_ids], axis=1).reshape(-1)
-    slots = wanted.shape[0]
-    capacity = 5 * (slots // devices) // 2
-    owner = wanted // rows_dev
-    local = wanted % rows_dev
-    onehot = (owner[:, None] == jnp.arange(devices, dtype=jnp.int32)[None, :]).astype(jnp.int32)
-    rank = jnp.sum(jnp.cumsum(onehot, axis=0) * onehot, axis=1) - 1
-    place = owner * capacity + rank
-    request = jnp.zeros((devices * capacity,), jnp.int32).at[place].set(local)
-    asked = lax.all_to_all(
-        request.reshape(devices, capacity),
-        ("user", "item"),
-        split_axis=0,
-        concat_axis=0,
-        tiled=True,
-    )
-    found = table[asked]
-    asked, fetched = (
-        asked,
-        lax.all_to_all(found, ("user", "item"), split_axis=0, concat_axis=0, tiled=True),
-    )
-    rows = fetched.reshape(devices * capacity, width)[place].reshape(users_here, -1, width)
-    grad_flat = attention(rows.reshape(-1, width), hist_len, teacher, w_query, w_key, w_value)
-    outgoing = jnp.zeros((devices * capacity, width), jnp.bfloat16).at[place].set(grad_flat)
-    arrived = lax.all_to_all(
-        outgoing.reshape(devices, capacity, width),
-        ("user", "item"),
-        split_axis=0,
-        concat_axis=0,
-        tiled=True,
-    )
-    grad_table = jnp.zeros((rows_dev, width), jnp.float32)
-    return grad_table.at[asked.reshape(-1)].add(arrived.reshape(-1, width).astype(jnp.float32))
+    rows, place, asked = fetch(cand_ids, hist_ids, table)
+    grads = attention(rows, hist_len, teacher, w_query, w_key, w_value)
+    return give_back(grads, place, asked)
 
 
 def solution(mesh):

time: 210 us -> 135 us (0.64)
  the two profiles are of different devices: /device:TPU:1 before, /device:TPU:0 now
where the time goes in v2:
time: 135 us
  Pallas kernels  125 us (93%)
  local copies, waits for them, and re-layouts  8.56 us (6%)
    pallas_call x1, Pallas kernels, fetch(): pl.pallas_call(fetch_kernel, out_shape=[jax.ShapeDtypeStruct((ROWS, WIDTH...  57.2 us
    pallas_call x1, Pallas kernels, give_back(): pl.pallas_call(give_back_kernel, out_shape=jax.ShapeDtypeStruct((TABLE_RO...  50.4 us
    pallas_call x1, Pallas kernels, attention(): pl.pallas_call(attention_kernel, out_shape=jax.ShapeDtypeStruct((CAND + H...  17.9 us
    unnamed x13, local copies, waits for them, and re-layouts  7.68 us

profile of v2, /device:TPU:0, one launch (start us, length us, event | category | flops | bytes accessed | tf_op | source)
XLA Modules:
  0.0 134.7 jit_solution(18342642368891959579)
XLA Ops:
  0.7 0.9 broadcast_in_dim.8.teacher_ref
  1.5 0.0 copy-start
  1.5 1.6 %copy-done = bf16[4096,256]{1,0:T(8,128)(2,1)S(1)} copy-done((bf16[4096,256]{1,0:T(8,128)(2,1)S(1)}, bf16[4096,256]{1,0:T(8,128)(2,1)}, u32[]{:S(2)}) %copy-start) | copy-done | bytes 2097176
  3.1 0.0 copy-start.1
  3.1 0.7 copy-done.1
  3.8 0.0 copy-start.2
  3.8 0.7 copy-done.2
  4.5 57.2 %fetch.1 = (bf16[2048,256]{1,0:T(8,128)(2,1)S(1)}, f32[1,2048]{1,0:T(1,128)S(1)}, f32[16,8,128]{2,1,0:T(8,128)S(1)}) custom-call(s32[1,1024]{1,0:T(1,128)S(1)} %copy-done.1, s32[1,1024]{1,0:T(1,128)S(1)} %copy-done.2, bf16[4096,256]{1,0:T(8,128)(2,1)S(1)} %copy-done), custom_call_target="tpu_custom_call" | custom-call | tf_op jit(solution)/shard_map/fetch/pallas_call | solution.py:285
  61.7 0.0 copy-start.3
  61.7 0.9 copy-done.3
  62.6 0.0 copy-start.4
  62.6 0.9 copy-done.4
  63.5 0.0 copy-start.5
  63.5 0.9 copy-done.5
  64.4 17.9 %attention.1.grad_ref = bf16[2048,256]{1,0:T(8,128)(2,1)S(1)} custom-call(s32[1]{0:T(128)S(6)} %copy.10.len_ref, bf16[2048,256]{1,0:T(8,128)(2,1)S(1)} %get-tuple-element.8.rows_ref, f32[1024,128]{1,0:T(8,128)S(1)} %broadcast_in_dim.8.teacher_ref, bf16[256,256]{1,0:T(8,128)(2,1)S(1)} %copy-done.3, bf16[256,256]{1,0:T(8,128)(2,1)S(1)} %copy-done.4, ...), custom_call_target="tpu_custom_call" | custom-call | flops 4000000000 | bytes 3145728 | tf_op jit(solution)/shard_map/attention/pallas_call | solution.py:103
  82.4 50.4 %give_back.1 = f32[4096,256]{1,0:T(8,128)S(1)} custom-call(bf16[2048,256]{1,0:T(8,128)(2,1)S(1)} %attention.1.grad_ref, f32[1,2048]{1,0:T(1,128)S(1)} %get-tuple-element.9.place_ref, f32[16,8,128]{2,1,0:T(8,128)S(1)} %get-tuple-element.10.asked_ref), custom_call_target="tpu_custom_call" | custom-call | tf_op jit(solution)/shard_map/give_back/pallas_call | solution.py:379
  132.7 2.0 %copy.11 = f32[4096,256]{1,0:T(8,128)} copy(f32[4096,256]{1,0:T(8,128)S(1)} %give_back.1) | data formatting | bytes 8388608
Async XLA Ops:
  1.5 1.6 %copy-start = (bf16[4096,256]{1,0:T(8,128)(2,1)S(1)}, bf16[4096,256]{1,0:T(8,128)(2,1)}, u32[]{:S(2)}) copy-start(bf16[4096,256]{1,0:T(8,128)(2,1)} %table_ref.1) | copy-start | bytes 6291460
  3.1 0.7 copy-start.1
  3.8 0.7 copy-start.2
  61.7 0.9 copy-start.3
  62.6 0.9 copy-start.4
  63.5 0.9 copy-start.5

commit v3 on v1

--- a/solution.py
+++ b/solution.py
@@ -30,9 +30,8 @@
     return lax.dot_general(a, b, (((1,), (1,)), ((), ())), preferred_element_type=jnp.float32)
 
 
-def attention_kernel(len_ref, rows_ref, teacher_ref, wq_ref, wk_ref, wv_ref, out_ref, q_s, kt_s, vt_s, vk1_s, cq_s, ee_s, xx_s, dvk_s):
+def attend(length, rows_ref, teacher_ref, wq_ref, wk_ref, wv_ref, out_ref, kt_s, vt_s, vk1_s, cq_s, ee_s, xx_s, dvk_s):
     half = jnp.bfloat16
-    length = len_ref[0]
     live = lax.broadcasted_iota(jnp.int32, (HIST, 128), 0) < length
     live2 = jnp.concatenate([live, live], axis=1)
     hist = jnp.where(live2, rows_ref[CAND:, :], jnp.zeros((), half))
@@ -42,7 +41,6 @@
     vt_s[...] = values.T
     cand = rows_ref[:CAND, :]
     query = dot(cand, wq_ref[...]).astype(half)
-    q_s[...] = query
     ones = jnp.where(live, 1.0, 0.0).astype(half)
     for h in range(HEADS):
         part = slice(h * HEAD, (h + 1) * HEAD)
@@ -97,69 +95,333 @@
     out_ref[CAND:, :] = jnp.where(live2, grad_hist, 0.0).astype(half)
 
 
-def attention(rows, length, teacher, w_query, w_key, w_value):
+USERS = 16
+ITEMS = 8
+PEERS = USERS * ITEMS
+CAP = 40
+TABLE_ROWS = 4096
+ROWS = CAND + HIST
+SUB = 6
+PART = SUB * CAP
+PAIR = 2 * SUB
+STEPS = 11
+PADDED = STEPS * PAIR
+LAG = 5
+LEAD = 11
+MESH = pl.DeviceIdType.MESH
+
+
+def partner(k, sign):
+    dz = k % 4
+    dx = (k // 4 + dz) % 4
+    dy = (k // 16 + dz) % 4
+    dc = k // 64
+    user = lax.axis_index("user")
+    item = lax.axis_index("item")
+    z = (user // 4 + 4 + sign * dz) % 4
+    x = (user % 4 + 4 + sign * dx) % 4
+    y = (item // 2 + 4 + sign * dy) % 4
+    c = (item % 2 + dc) % 2
+    return z * 4 + x, y * 2 + c
+
+
+def partner_index(owner):
+    user = lax.axis_index("user")
+    item = lax.axis_index("item")
+    dz = (user // 4 - owner // 32) & 3
+    a = (user % 4 - owner // 8 - dz) & 3
+    b = (item // 2 - owner // 2 - dz) & 3
+    dc = (item - owner) & 1
+    return dc * 64 + b * 16 + a * 4 + dz
+
+
+def linear(where):
+    return where[0] * ITEMS + where[1]
+
+
+def one_hot(match):
+    return jnp.where(match, 1.0, 0.0).astype(jnp.bfloat16)
+
+
+def keep(match, value):
+    return jnp.where(match, value, jnp.zeros((), value.dtype))
+
+
+def greet():
+    user = lax.axis_index("user")
+    item = lax.axis_index("item")
+    barrier = pltpu.get_barrier_semaphore()
+    for step in range(1, ITEMS):
+        pl.semaphore_signal(barrier, inc=1, device_id=(user, (item + step) % ITEMS), device_id_type=MESH)
+    for step in range(1, USERS):
+        pl.semaphore_signal(barrier, inc=1, device_id=((user + step) % USERS, item), device_id_type=MESH)
+    return barrier
+
+
+def requests(cand_ref, hist_ref, high_ref, low_ref):
     half = jnp.bfloat16
+    rows = lax.broadcasted_iota(jnp.int32, (PEERS, 256), 0)
+    slot = lax.broadcasted_iota(jnp.int32, (64, 256), 0).astype(jnp.float32)
+    upper = one_hot(lax.broadcasted_iota(jnp.int32, (256, 256), 0) < lax.broadcasted_iota(jnp.int32, (256, 256), 1))
+    taken = jnp.zeros((PEERS, 1), jnp.float32)
+    wanted = jnp.zeros((PEERS, 128), jnp.float32)
+    for c in range(ROWS // 256):
+        at = c * 256
+        ids = cand_ref[:, at:at + 256] if at < CAND else hist_ref[:, at - CAND:at - CAND + 256]
+        owner = ids // TABLE_ROWS
+        local = ids % TABLE_ROWS
+        full = jnp.where(rows == owner, 1.0, 0.0)
+        chosen = full.astype(half)
+        rank = jnp.sum(full * (dot(chosen, upper) + taken), axis=0, keepdims=True)
+        taken = taken + jnp.sum(full, axis=1, keepdims=True)
+        k = partner_index(owner)
+        part = (k * 43) // 256
+        high_ref[:, at:at + 256] = part.astype(jnp.float32)
+        low_ref[:, at:at + 256] = ((k - part * SUB) * CAP).astype(jnp.float32) + rank
+        mine = slot == rank
+        upper_half = (local // 64).astype(jnp.float32)
+        lower_half = (local % 64).astype(jnp.float32)
+        split = jnp.concatenate([jnp.where(mine, upper_half, 0.0), jnp.where(mine, lower_half, 0.0)], axis=0).astype(half)
+        wanted = wanted + dot_nt(chosen, split)
+    return jnp.concatenate([wanted[:, :64] * 64.0 + wanted[:, 64:], jnp.zeros((PEERS, 64), jnp.float32)], axis=1)
+
+
+def send_part(n, found, buffer, landing, send_sem, recv_sem, sign):
+    for kk in range(PAIR):
+        k = n * PAIR + kk
+        buffer[k] = found[kk * CAP:(kk + 1) * CAP].astype(jnp.bfloat16)
+
+        def start():
+            pltpu.make_async_remote_copy(
+                src_ref=buffer.at[k], dst_ref=landing.at[k], send_sem=send_sem, recv_sem=recv_sem.at[n],
+                device_id=partner(k, sign), device_id_type=MESH).start()
+
+        if kk == 0:
+            pl.when(n > 0)(start)
+        elif kk < PEERS - (STEPS - 1) * PAIR:
+            start()
+        else:
+            pl.when(n < STEPS - 1)(start)
+
+
+def landed(n, buffer, landing, recv_sem):
+    def wait(first, count):
+        here = pl.ds(first, count)
+        pltpu.make_async_copy(buffer.at[here], landing.at[here], recv_sem.at[n]).wait()
+
+    @pl.when(n == 0)
+    def _():
+        wait(1, PAIR - 1)
+
+    @pl.when(jnp.logical_and(n > 0, n < STEPS - 1))
+    def _():
+        wait(n * PAIR, PAIR)
+
+    @pl.when(n == STEPS - 1)
+    def _():
+        wait((STEPS - 1) * PAIR, PEERS - (STEPS - 1) * PAIR)
+
+
+def slabs(n, landing):
+    half = jnp.bfloat16
+    tail = jnp.zeros((256 - PART, WIDTH), half)
+    parts = []
+    for s in range(2):
+        part = landing[pl.ds(n * PAIR + s * SUB, SUB)].astype(jnp.float32).reshape(PART, WIDTH).astype(half)
+        parts += [part, tail]
+    return jnp.concatenate(parts, axis=0)
+
+
+def number(value, shape):
+    return jnp.broadcast_to(jnp.asarray(value, jnp.int32).astype(jnp.float32), shape).astype(jnp.bfloat16)
+
+
+def ranker_kernel(
+    len_ref, cand_ref, hist_ref, teacher_ref, table_any, wq_any, wk_any, wv_any, out_ref,
+    table_ref, wq_ref, wk_ref, wv_ref, high_ref, low_ref, want_s, item_out, item_in, user_out, asked_ref, wide_s,
+    send_s, recv_s, back_s, home_s, low_col, high_col, low_row, acc_s, rows_ref, grad_ref, aim_s,
+    kt_s, vt_s, vk1_s, cq_s, ee_s, xx_s, dvk_s,
+    local, isend, irecv, usend, urecv, rsend, rrecv, gsend, grecv,
+):
+    half = jnp.bfloat16
+    full = jnp.float32
+    user = lax.axis_index("user")
+    item = lax.axis_index("item")
+    barrier = greet()
+    loads = [
+        pltpu.make_async_copy(src, dst, local.at[n])
+        for n, (src, dst) in enumerate([(table_any, table_ref), (wq_any, wq_ref), (wk_any, wk_ref), (wv_any, wv_ref)])
+    ]
+    for load in loads:
+        load.start()
+    want_s[...] = requests(cand_ref, hist_ref, high_ref, low_ref)
+    for i in range(ITEMS):
+        item_out[i] = want_s[pl.ds(i, USERS, stride=ITEMS), :]
+    pl.semaphore_wait(barrier, USERS + ITEMS - 2)
+    for step in range(1, ITEMS):
+        to = (item + step) % ITEMS
+        pltpu.make_async_remote_copy(
+            src_ref=item_out.at[to], dst_ref=item_in.at[item], send_sem=isend, recv_sem=irecv,
+            device_id=(user, to), device_id_type=MESH).start()
+    item_in[item] = item_out[item]
+    low = jnp.broadcast_to(low_ref[...], (128, ROWS)).T
+    lane = lax.broadcasted_iota(jnp.int32, (ROWS, 128), 1).astype(full)
+    low_col[:, :128] = one_hot(low == lane)
+    low_col[:, 128:] = one_hot(low == lane + 128.0)
+    high_col[...] = jnp.broadcast_to(high_ref[...], (128, ROWS)).T.astype(half)
+    low_row[...] = one_hot(low_ref[...] == lax.broadcasted_iota(jnp.int32, (PART, ROWS), 0).astype(full))
+    pltpu.make_async_copy(item_out.at[pl.ds(1, ITEMS - 1)], item_in.at[pl.ds(1, ITEMS - 1)], irecv).wait()
+    for u in range(USERS):
+        user_out[u] = jnp.concatenate([item_in[i, u:u + 1, :] for i in range(ITEMS)], axis=0)
+    for step in range(1, USERS):
+        to = (user + step) % USERS
+        pltpu.make_async_remote_copy(
+            src_ref=user_out.at[to], dst_ref=asked_ref.at[user], send_sem=usend, recv_sem=urecv,
+            device_id=(to, item), device_id_type=MESH).start()
+    asked_ref[user] = user_out[user]
+    acc_s[...] = jnp.zeros_like(acc_s)
+    aim_s[...] = jnp.broadcast_to(teacher_ref[...], (128, CAND)).T
+    out_ref[...] = jnp.zeros_like(out_ref)
+    for spare in range(PEERS, PADDED):
+        recv_s[spare] = jnp.zeros((CAP, WIDTH), half)
+        home_s[spare] = jnp.zeros((CAP, WIDTH), half)
+    pltpu.make_async_copy(user_out.at[pl.ds(1, USERS - 1)], asked_ref.at[pl.ds(1, USERS - 1)], urecv).wait()
+    loads[0].wait()
+    turned = asked_ref[...].reshape(PEERS, 128).T
+    for p in range(PEERS):
+        wide_s[p] = jnp.broadcast_to(turned[:CAP, p:p + 1], (CAP, 128))
+    lane = lax.broadcasted_iota(jnp.int32, (2 * PART, 128), 1).astype(full)
+
+    def give(n, carry):
+        ids = jnp.concatenate([wide_s[linear(partner(n * PAIR + kk, 1))] for kk in range(PAIR)], axis=0)
+        high = jnp.floor(ids * (1.0 / 256.0))
+        low = ids - high * 256.0
+        low = jnp.concatenate([one_hot(low == lane), one_hot(low == lane + 128.0)], axis=1)
+        high = high.astype(half)
+        high = jnp.concatenate([high, high], axis=1)
+        found = jnp.zeros((2 * PART, WIDTH), full)
+        for c in range(TABLE_ROWS // 256):
+            found = found + dot(keep(high == number(c, (1, 1)), low), table_ref[c * 256:(c + 1) * 256, :])
+        send_part(n, found, send_s, recv_s, rsend, rrecv, 1)
+        return carry
+
+    def take(n, carry):
+        landed(n, send_s, recv_s, rrecv)
+        slab = slabs(n, recv_s)
+        for r in range(ROWS // 512):
+            at = slice(r * 512, (r + 1) * 512)
+            high = high_col[at, :]
+            high = jnp.concatenate([high, high], axis=1)
+            low = low_col[at, :]
+            picked = jnp.concatenate([keep(high == number(2 * n + s, (1, 256)), low) for s in range(2)], axis=1)
+            acc_s[at, :] += dot(picked, slab)
+        return carry
+
+    lax.fori_loop(0, LEAD, give, 0)
+    recv_s[0] = send_s[0]
+    lax.fori_loop(LEAD, STEPS, lambda n, carry: take(n - LEAD, give(n, carry)), 0)
+    lax.fori_loop(STEPS - LEAD, STEPS, take, 0)
+    rows_ref[...] = acc_s[...].astype(half)
+    for load in loads[1:]:
+        load.wait()
+    attend(len_ref[0], rows_ref, aim_s, wq_ref, wk_ref, wv_ref, grad_ref, kt_s, vt_s, vk1_s, cq_s, ee_s, xx_s, dvk_s)
+    high_row = jnp.broadcast_to(high_ref[...], (16, ROWS))
+
+    def give_back(n, carry):
+        found = []
+        for s in range(2):
+            match = one_hot(high_row == (2 * n + s).astype(full))
+            part = jnp.zeros((PART, WIDTH), full)
+            for c in range(ROWS // 512):
+                at = slice(c * 512, (c + 1) * 512)
+                mine = jnp.concatenate([match[:, at]] * (PART // 16), axis=0)
+                part = part + dot(mine * low_row[:, at], grad_ref[at, :])
+            found.append(part)
+        send_part(n, jnp.concatenate(found, axis=0), back_s, home_s, gsend, grecv, -1)
+        return carry
+
+    deep = lax.broadcasted_iota(jnp.int32, (256, 512), 0).astype(full)
+
+    def take_back(n, carry):
+        landed(n, back_s, home_s, grecv)
+        slab = slabs(n, home_s)
+        ids = []
+        for kk in range(PAIR):
+            source = partner(n * PAIR + kk, 1)
+            ids.append(asked_ref[source[0], pl.ds(source[1], 1), :][:, :CAP])
+            if kk % SUB == SUB - 1:
+                ids.append(jnp.zeros((1, 256 - PART), full))
+        ids = jnp.concatenate(ids, axis=1)
+        high = jnp.floor(ids * (1.0 / 256.0))
+        low = one_hot(ids - high * 256.0 == deep)
+        high = jnp.broadcast_to(high, (16, 512))
+        for c in range(0, TABLE_ROWS // 256, 2):
+            picked = []
+            for d in range(2):
+                mine = one_hot(high == float(c + d))
+                picked.append(jnp.concatenate([mine] * 16, axis=0) * low)
+            at = slice(c * 256, (c + 2) * 256)
+            out_ref[at, :] += dot(jnp.concatenate(picked, axis=0), slab)
+        return carry
+
+    lax.fori_loop(0, LAG, give_back, 0)
+    home_s[0] = back_s[0]
+    lax.fori_loop(LAG, STEPS, lambda n, carry: take_back(n - LAG, give_back(n, carry)), 0)
+    lax.fori_loop(STEPS - LAG, STEPS, take_back, 0)
+    pltpu.make_async_copy(back_s.at[pl.ds(1, PEERS - 1)], home_s.at[pl.ds(1, PEERS - 1)], gsend).wait()
+    pltpu.make_async_copy(item_out.at[pl.ds(1, ITEMS - 1)], item_in.at[pl.ds(1, ITEMS - 1)], isend).wait()
+    pltpu.make_async_copy(user_out.at[pl.ds(1, USERS - 1)], asked_ref.at[pl.ds(1, USERS - 1)], usend).wait()
+    pltpu.make_async_copy(send_s.at[pl.ds(1, PEERS - 1)], recv_s.at[pl.ds(1, PEERS - 1)], rsend).wait()
+
+
+def body(cand_ids, hist_ids, hist_len, teacher, table, w_query, w_key, w_value):
+    half = jnp.bfloat16
+    full = jnp.float32
     space = pl.BlockSpec(memory_space=pltpu.VMEM)
+    anywhere = pl.BlockSpec(memory_space=pltpu.HBM)
+    sem = pltpu.SemaphoreType.DMA
+    vmem = pltpu.VMEM
     return pl.pallas_call(
-        attention_kernel,
-        out_shape=jax.ShapeDtypeStruct((CAND + HIST, WIDTH), half),
-        in_specs=[pl.BlockSpec(memory_space=pltpu.SMEM)] + [space] * 5,
+        ranker_kernel,
+        out_shape=pltpu.VMEM((TABLE_ROWS, WIDTH), full),
+        in_specs=[pl.BlockSpec(memory_space=pltpu.SMEM)] + [space] * 3 + [anywhere] * 4,
         out_specs=space,
         scratch_shapes=[
-            pltpu.VMEM((CAND, WIDTH), half),
-            pltpu.VMEM((WIDTH, HIST), half),
-            pltpu.VMEM((WIDTH, HIST), half),
-            pltpu.VMEM((HEADS, HIST, 256), half),
-            pltpu.VMEM((HEADS, CAND, 128), half),
-            pltpu.VMEM((HEADS, 2 * BLOCK, HIST), half),
-            pltpu.VMEM((HEADS, 2 * BLOCK, 128), half),
-            pltpu.VMEM((HEADS, 128, HIST), jnp.float32),
+            vmem((TABLE_ROWS, WIDTH), half),
+            vmem((WIDTH, WIDTH), half),
+            vmem((WIDTH, WIDTH), half),
+            vmem((WIDTH, WIDTH), half),
+            vmem((1, ROWS), full),
+            vmem((1, ROWS), full),
+            vmem((PEERS, 128), full),
+            vmem((ITEMS, USERS, 128), full),
+            vmem((ITEMS, USERS, 128), full),
+            vmem((USERS, ITEMS, 128), full),
+            vmem((USERS, ITEMS, 128), full),
+            vmem((PEERS, CAP, 128), full),
+            vmem((PADDED, CAP, WIDTH), half),
+            vmem((PADDED, CAP, WIDTH), half),
+            vmem((PADDED, CAP, WIDTH), half),
+            vmem((PADDED, CAP, WIDTH), half),
+            vmem((ROWS, 256), half),
+            vmem((ROWS, 128), half),
+            vmem((PART, ROWS), half),
+            vmem((ROWS, WIDTH), full),
+            vmem((ROWS, WIDTH), half),
+            vmem((ROWS, WIDTH), half),
+            vmem((CAND, 128), full),
+            vmem((WIDTH, HIST), half),
+            vmem((WIDTH, HIST), half),
+            vmem((HEADS, HIST, 256), half),
+            vmem((HEADS, CAND, 128), half),
+            vmem((HEADS, 2 * BLOCK, HIST), half),
+            vmem((HEADS, 2 * BLOCK, 128), half),
+            vmem((HEADS, 128, HIST), full),
+            sem((4,)), sem(()), sem(()), sem(()), sem(()), sem(()), sem((STEPS,)), sem(()), sem((STEPS,)),
         ],
-        compiler_params=pltpu.CompilerParams(vmem_limit_bytes=48 * 2**20),
-        cost_estimate=pl.CostEstimate(flops=4 * 10**9, bytes_accessed=3 * 2**20, transcendentals=4 * 2**20),
-        name="attention",
-    )(length, rows, jnp.broadcast_to(teacher.reshape(CAND, 1), (CAND, 128)), w_query, w_key, w_value)
-
-
-def body(cand_ids, hist_ids, hist_len, teacher, table, w_query, w_key, w_value):
-    rows_dev, width = table.shape
-    users_here, cand = cand_ids.shape
-    user_count = lax.axis_size("user")
-    item_count = lax.axis_size("item")
-    devices = user_count * item_count
-    wanted = jnp.concatenate([cand_ids, hist_ids], axis=1).reshape(-1)
-    slots = wanted.shape[0]
-    capacity = 5 * (slots // devices) // 2
-    owner = wanted // rows_dev
-    local = wanted % rows_dev
-    onehot = (owner[:, None] == jnp.arange(devices, dtype=jnp.int32)[None, :]).astype(jnp.int32)
-    rank = jnp.sum(jnp.cumsum(onehot, axis=0) * onehot, axis=1) - 1
-    place = owner * capacity + rank
-    request = jnp.zeros((devices * capacity,), jnp.int32).at[place].set(local)
-    asked = lax.all_to_all(
-        request.reshape(devices, capacity),
-        ("user", "item"),
-        split_axis=0,
-        concat_axis=0,
-        tiled=True,
-    )
-    found = table[asked]
-    asked, fetched = (
-        asked,
-        lax.all_to_all(found, ("user", "item"), split_axis=0, concat_axis=0, tiled=True),
-    )
-    rows = fetched.reshape(devices * capacity, width)[place].reshape(users_here, -1, width)
-    grad_flat = attention(rows.reshape(-1, width), hist_len, teacher, w_query, w_key, w_value)
-    outgoing = jnp.zeros((devices * capacity, width), jnp.bfloat16).at[place].set(grad_flat)
-    arrived = lax.all_to_all(
-        outgoing.reshape(devices, capacity, width),
-        ("user", "item"),
-        split_axis=0,
-        concat_axis=0,
-        tiled=True,
-    )
-    grad_table = jnp.zeros((rows_dev, width), jnp.float32)
-    return grad_table.at[asked.reshape(-1)].add(arrived.reshape(-1, width).astype(jnp.float32))
+        compiler_params=pltpu.CompilerParams(collective_id=0, has_side_effects=True, vmem_limit_bytes=56 * 2**20),
+        name="ranker",
+    )(hist_len, cand_ids, hist_ids, teacher, *(pltpu.with_memory_space_constraint(x, pltpu.HBM) for x in (table, w_query, w_key, w_value)))
 
 
 def solution(mesh):

time: 210 us -> 111 us (0.53)
  Pallas kernels: 18 us -> 108 us
  waiting for transfers between devices: 69.6 us -> 0 us
  local copies, waits for them, and re-layouts: 54.8 us -> 2.02 us
  other arithmetic: 34 us -> 0 us
  blocking collectives: 20.9 us -> 0 us
  starting transfers between devices: 10.8 us -> 0 us
    pallas_call x1, Pallas kernels: 18 us -> 108 us  [body(): pl.pallas_call(ranker_kernel, out_shape=pltpu.VMEM((TABLE_ROWS, WIDTH), f...]
    all_to_all x2 -> x0, waiting for transfers between devices: 69.6 us -> none  [the longest x1 35.3 us: body(): lax.all_to_all(found, ('user', 'item'), split_axis=0, concat_axis=0, tile...]
    scatter-add x1 -> x0, other arithmetic: 32 us -> none  [body(): grad_table.at[asked.reshape(-1)]]
    gather x2 -> x0, local copies, waits for them, and re-layouts: 29.9 us -> none  [the longest x1 21.1 us: body(): found = table[asked]]
    all_to_all x1 -> x0, blocking collectives: 20.9 us -> none  [body(): lax.all_to_all(request.reshape(devices, capacity), ('user', 'item'), spli...]
    scatter x2 -> x0, local copies, waits for them, and re-layouts: 19.6 us -> none  [the longest x1 11.5 us: body(): jnp.zeros((devices * capacity, width), jnp.bfloat16).at[place]]
    all_to_all x2 -> x0, starting transfers between devices: 10.8 us -> none  [the longest x1 5.57 us: body(): lax.all_to_all(outgoing.reshape(devices, capacity, width), ('user', 'item...]
  transfers between devices with their start and end apart: 2 -> 0, of which waited for: 2 -> 0; matrix products, arithmetic and copies ran while one was open for 1% -> 0% of each run, Pallas kernels for 0% -> 0%
where the time goes in v3:
time: 111 us; the launch traced here: 110 us
  Pallas kernels  108 us (97%)
  local copies, waits for them, and re-layouts  2.02 us (2%)
    pallas_call x1, Pallas kernels, body(): pl.pallas_call(ranker_kernel, out_shape=pltpu.VMEM((TABLE_ROWS, WIDTH), f...  108 us

profile of v3, /device:TPU:1, one launch (start us, length us, event | category | flops | bytes accessed | tf_op | source)
XLA Modules:
  0.0 110.3 jit_solution(9993970837622420476)
XLA Ops:
  0.7 107.6 %ranker.1 = f32[4096,256]{1,0:T(8,128)S(1)} custom-call(s32[1]{0:T(128)S(6)} %copy.11.len_ref, s32[1,1024]{1,0:T(1,128)} %cand_ref.1, s32[1,1024]{1,0:T(1,128)} %hist_ref.1, f32[1,1024]{1,0:T(1,128)} %teacher_ref.1, bf16[4096,256]{1,0:T(8,128)(2,1)} %table_any.1, bf16[256,256]{1,0:T(8,128)(2,1)} %wq_any.1, bf16[256,256]{1,0:T(8,128)(2,1)} %wk_any.1, ...), custom_call_target="tpu_custom_call" | custom-call | tf_op jit(solution)/shard_map/ranker/pallas_call | solution.py:384
  108.3 2.0 %copy.10 = f32[4096,256]{1,0:T(8,128)} copy(f32[4096,256]{1,0:T(8,128)S(1)} %ranker.1) | data formatting | bytes 8388608

commit v4 on v3

--- a/solution.py
+++ b/solution.py
@@ -15,7 +15,7 @@
 HIST = 1024
 WIDTH = 256
 HEAD = 64
-BLOCK = 256
+BLOCK = 512
 
 
 def dot(a, b):
@@ -264,12 +264,6 @@
             src_ref=item_out.at[to], dst_ref=item_in.at[item], send_sem=isend, recv_sem=irecv,
             device_id=(user, to), device_id_type=MESH).start()
     item_in[item] = item_out[item]
-    low = jnp.broadcast_to(low_ref[...], (128, ROWS)).T
-    lane = lax.broadcasted_iota(jnp.int32, (ROWS, 128), 1).astype(full)
-    low_col[:, :128] = one_hot(low == lane)
-    low_col[:, 128:] = one_hot(low == lane + 128.0)
-    high_col[...] = jnp.broadcast_to(high_ref[...], (128, ROWS)).T.astype(half)
-    low_row[...] = one_hot(low_ref[...] == lax.broadcasted_iota(jnp.int32, (PART, ROWS), 0).astype(full))
     pltpu.make_async_copy(item_out.at[pl.ds(1, ITEMS - 1)], item_in.at[pl.ds(1, ITEMS - 1)], irecv).wait()
     for u in range(USERS):
         user_out[u] = jnp.concatenate([item_in[i, u:u + 1, :] for i in range(ITEMS)], axis=0)
@@ -279,12 +273,6 @@
             src_ref=user_out.at[to], dst_ref=asked_ref.at[user], send_sem=usend, recv_sem=urecv,
             device_id=(to, item), device_id_type=MESH).start()
     asked_ref[user] = user_out[user]
-    acc_s[...] = jnp.zeros_like(acc_s)
-    aim_s[...] = jnp.broadcast_to(teacher_ref[...], (128, CAND)).T
-    out_ref[...] = jnp.zeros_like(out_ref)
-    for spare in range(PEERS, PADDED):
-        recv_s[spare] = jnp.zeros((CAP, WIDTH), half)
-        home_s[spare] = jnp.zeros((CAP, WIDTH), half)
     pltpu.make_async_copy(user_out.at[pl.ds(1, USERS - 1)], asked_ref.at[pl.ds(1, USERS - 1)], urecv).wait()
     loads[0].wait()
     turned = asked_ref[...].reshape(PEERS, 128).T
@@ -319,6 +307,18 @@
 
     lax.fori_loop(0, LEAD, give, 0)
     recv_s[0] = send_s[0]
+    low = jnp.broadcast_to(low_ref[...], (128, ROWS)).T
+    column = lax.broadcasted_iota(jnp.int32, (ROWS, 128), 1).astype(full)
+    low_col[:, :128] = one_hot(low == column)
+    low_col[:, 128:] = one_hot(low == column + 128.0)
+    high_col[...] = jnp.broadcast_to(high_ref[...], (128, ROWS)).T.astype(half)
+    low_row[...] = one_hot(low_ref[...] == lax.broadcasted_iota(jnp.int32, (PART, ROWS), 0).astype(full))
+    acc_s[...] = jnp.zeros_like(acc_s)
+    aim_s[...] = jnp.broadcast_to(teacher_ref[...], (128, CAND)).T
+    out_ref[...] = jnp.zeros_like(out_ref)
+    for spare in range(PEERS, PADDED):
+        recv_s[spare] = jnp.zeros((CAP, WIDTH), half)
+        home_s[spare] = jnp.zeros((CAP, WIDTH), half)
     lax.fori_loop(LEAD, STEPS, lambda n, carry: take(n - LEAD, give(n, carry)), 0)
     lax.fori_loop(STEPS - LEAD, STEPS, take, 0)
     rows_ref[...] = acc_s[...].astype(half)

time: 111 us -> 110 us (level)
  no operation moved by 1% of the time
where the time goes in v4:
time: 110 us
  Pallas kernels  107 us (97%)
  local copies, waits for them, and re-layouts  2.02 us (2%)
    pallas_call x1, Pallas kernels, body(): pl.pallas_call(ranker_kernel, out_shape=pltpu.VMEM((TABLE_ROWS, WIDTH), f...  107 us

profile of v4, /device:TPU:1, one launch (start us, length us, event | category | flops | bytes accessed | tf_op | source)
XLA Modules:
  0.0 109.6 jit_solution(4141507067214426925)
XLA Ops:
  0.7 106.9 %ranker.1 = f32[4096,256]{1,0:T(8,128)S(1)} custom-call(s32[1]{0:T(128)S(6)} %copy.11.len_ref, s32[1,1024]{1,0:T(1,128)} %cand_ref.1, s32[1,1024]{1,0:T(1,128)} %hist_ref.1, f32[1,1024]{1,0:T(1,128)} %teacher_ref.1, bf16[4096,256]{1,0:T(8,128)(2,1)} %table_any.1, bf16[256,256]{1,0:T(8,128)(2,1)} %wq_any.1, bf16[256,256]{1,0:T(8,128)(2,1)} %wk_any.1, ...), custom_call_target="tpu_custom_call" | custom-call | tf_op jit(solution)/shard_map/ranker/pallas_call | solution.py:384
  107.6 2.0 %copy.10 = f32[4096,256]{1,0:T(8,128)} copy(f32[4096,256]{1,0:T(8,128)S(1)} %ranker.1) | data formatting | bytes 8388608

commit v5 on v4

--- a/solution.py
+++ b/solution.py
@@ -186,10 +186,10 @@
     return jnp.concatenate([wanted[:, :64] * 64.0 + wanted[:, 64:], jnp.zeros((PEERS, 64), jnp.float32)], axis=1)
 
 
-def send_part(n, found, buffer, landing, send_sem, recv_sem, sign):
-    for kk in range(PAIR):
+def send_part(n, found, buffer, landing, send_sem, recv_sem, sign, first=0, count=PAIR):
+    for kk in range(first, first + count):
         k = n * PAIR + kk
-        buffer[k] = found[kk * CAP:(kk + 1) * CAP].astype(jnp.bfloat16)
+        buffer[k] = found[(kk - first) * CAP:(kk - first + 1) * CAP].astype(jnp.bfloat16)
 
         def start():
             pltpu.make_async_remote_copy(
@@ -328,7 +328,6 @@
     high_row = jnp.broadcast_to(high_ref[...], (16, ROWS))
 
     def give_back(n, carry):
-        found = []
         for s in range(2):
             match = one_hot(high_row == (2 * n + s).astype(full))
             part = jnp.zeros((PART, WIDTH), full)
@@ -336,8 +335,7 @@
                 at = slice(c * 512, (c + 1) * 512)
                 mine = jnp.concatenate([match[:, at]] * (PART // 16), axis=0)
                 part = part + dot(mine * low_row[:, at], grad_ref[at, :])
-            found.append(part)
-        send_part(n, jnp.concatenate(found, axis=0), back_s, home_s, gsend, grecv, -1)
+            send_part(n, part, back_s, home_s, gsend, grecv, -1, s * SUB, SUB)
         return carry
 
     deep = lax.broadcasted_iota(jnp.int32, (256, 512), 0).astype(full)

time: 110 us -> 116 us (1.055)
  Pallas kernels: 107 us -> 112 us
    pallas_call x1, Pallas kernels: 107 us -> 112 us  [body(): pl.pallas_call(ranker_kernel, out_shape=pltpu.VMEM((TABLE_ROWS, WIDTH), f...]
where the time goes in v5:
time: 116 us; the launch traced here: 115 us
  Pallas kernels  112 us (97%)
  local copies, waits for them, and re-layouts  2.02 us (2%)
    pallas_call x1, Pallas kernels, body(): pl.pallas_call(ranker_kernel, out_shape=pltpu.VMEM((TABLE_ROWS, WIDTH), f...  112 us

profile of v5, /device:TPU:1, one launch (start us, length us, event | category | flops | bytes accessed | tf_op | source)
XLA Modules:
  0.0 115.0 jit_solution(16840948433404327166)
XLA Ops:
  0.7 112.3 %ranker.1 = f32[4096,256]{1,0:T(8,128)S(1)} custom-call(s32[1]{0:T(128)S(6)} %copy.11.len_ref, s32[1,1024]{1,0:T(1,128)} %cand_ref.1, s32[1,1024]{1,0:T(1,128)} %hist_ref.1, f32[1,1024]{1,0:T(1,128)} %teacher_ref.1, bf16[4096,256]{1,0:T(8,128)(2,1)} %table_any.1, bf16[256,256]{1,0:T(8,128)(2,1)} %wq_any.1, bf16[256,256]{1,0:T(8,128)(2,1)} %wk_any.1, ...), custom_call_target="tpu_custom_call" | custom-call | tf_op jit(solution)/shard_map/ranker/pallas_call | solution.py:382
  112.9 2.0 %copy.10 = f32[4096,256]{1,0:T(8,128)} copy(f32[4096,256]{1,0:T(8,128)S(1)} %ranker.1) | data formatting | bytes 8388608
